TPU v7x, 256 devices: a whole 4x4x8 slice. The times are simulated.
256 devices in a mesh: gx: 4 (over x), gy: 8 (over y, core), gz: 8 (over z).
Axes of the slice: x: 4, y: 4, z: 8, core: 2. Of those that a mesh axis runs over, the one named last changes fastest.
Arguments:
- volume: bfloat16 [32, 128, 8192], P('gx', 'gy', 'gz'), may hold values from -6 to 6
- weight_top: bfloat16 [3, 3, 3, 64, 64], replicated, may hold values from -0.21875 to 0.21875
- weight_down_a: bfloat16 [3, 3, 3, 64, 128], replicated, may hold values from -0.21875 to 0.21875
- weight_down_b: bfloat16 [3, 3, 3, 128, 128], replicated, may hold values from -0.15625 to 0.15625
- weight_low_a: bfloat16 [3, 3, 3, 128, 256], replicated, may hold values from -0.15625 to 0.15625
- weight_low_b: bfloat16 [3, 3, 3, 256, 256], replicated, may hold values from -0.109375 to 0.109375
- weight_lift_low: bfloat16 [256, 2, 2, 2, 128], replicated, may hold values from -0.5 to 0.5
- weight_up_mid: bfloat16 [3, 3, 3, 256, 128], replicated, may hold values from -0.109375 to 0.109375
- weight_lift_top: bfloat16 [128, 2, 2, 2, 64], replicated, may hold values from -0.75 to 0.75
- weight_out: bfloat16 [3, 3, 3, 128, 64], replicated, may hold values from -0.15625 to 0.15625
Outputs:
- decoded: bfloat16 [32, 128, 8192], P('gx', 'gy', 'gz')
All inputs are finite; a program needn't handle non-finite values.
Results may differ from a plain program's by a relative error of at most 0.02.
Values may be sent and summed in bfloat16 or wider, within the bound.
A program may use at most 64 MiB of HBM per device.

v0:
```python
import jax
import jax.numpy as jnp
from jax import lax
from jax.sharding import PartitionSpec as P


def padded_2(cells, sides, width):
    for axis, dim in sides:
        count = lax.axis_size(axis)
        ends = count - 1
        head = lax.slice_in_dim(cells, 0, width, axis=dim)
        tail = lax.slice_in_dim(cells, cells.shape[dim] - width, cells.shape[dim], axis=dim)
        cells = jnp.concatenate(
            [
                lax.ppermute(tail, axis, [(i, (i + 1) % count) for i in range(ends)]),
                cells,
                lax.ppermute(head, axis, [((i + 1) % count, i) for i in range(ends)]),
            ],
            axis=dim,
        )
    return cells


def faces_pad(field):
    return padded_2(field, (("gx", 0), ("gy", 1), ("gz", 2)), 1)


def conv_valid(padded, weight):
    size_x = padded.shape[0] - 2
    size_y = padded.shape[1] - 2
    size_z = padded.shape[2] - 2
    inputs = padded.shape[3]
    outputs = weight.shape[4]
    stacked = jnp.concatenate(
        [padded[:, :, depth : depth + size_z, :] for depth in range(3)], axis=3
    )
    total = jnp.zeros((size_x * size_y * size_z, outputs), jnp.float32)
    for shift_x in range(3):
        for shift_y in range(3):
            piece = stacked[shift_x : shift_x + size_x, shift_y : shift_y + size_y].reshape(
                size_x * size_y * size_z, 3 * inputs
            )
            kernel = weight[shift_x, shift_y].reshape(3 * inputs, outputs)
            total = total + jnp.dot(piece, kernel, preferred_element_type=jnp.float32)
    return total.reshape(size_x, size_y, size_z, outputs)


def activate(total):
    return jnp.maximum(total, 0.0).astype(jnp.bfloat16)


def pool(field):
    size_x, size_y, size_z, channels = field.shape
    blocks = field.reshape(size_x // 2, 2, size_y // 2, 2, size_z // 2, 2, channels)
    return jnp.max(blocks, axis=(1, 3, 5))


def upsample(field, weight):
    size_x, size_y, size_z, inputs = field.shape
    outputs = weight.shape[4]
    product = jnp.dot(
        field.reshape(size_x * size_y * size_z, inputs),
        weight.reshape(inputs, 8 * outputs),
        preferred_element_type=jnp.float32,
    )
    product = product.astype(jnp.bfloat16).reshape(size_x, size_y, size_z, 2, 2, 2, outputs)
    return product.transpose(0, 3, 1, 4, 2, 5, 6).reshape(
        2 * size_x, 2 * size_y, 2 * size_z, outputs
    )


def coarse_faces_pad(field):
    return padded_2(field, (("gx", 0), ("gy", 1), ("gz", 2)), 1)


def body(
    volume,
    weight_top,
    weight_down_a,
    weight_down_b,
    weight_low_a,
    weight_low_b,
    weight_lift_low,
    weight_up_mid,
    weight_lift_top,
    weight_out,
):
    channels = weight_top.shape[3]
    size_x = volume.shape[0]
    size_y = volume.shape[1]
    size_z = volume.shape[2] // channels
    field = volume.reshape(size_x, size_y, size_z, channels)
    skip_top = activate(conv_valid(faces_pad(field), weight_top))
    first_mid = activate(conv_valid(faces_pad(pool(skip_top)), weight_down_a))
    skip_mid = activate(conv_valid(faces_pad(first_mid), weight_down_b))
    pool_low = pool(skip_mid)
    first_low = activate(conv_valid(coarse_faces_pad(pool_low), weight_low_a))
    coarse_out = activate(conv_valid(coarse_faces_pad(first_low), weight_low_b))
    lifted_mid = upsample(coarse_out, weight_lift_low)
    merged_mid = activate(
        conv_valid(faces_pad(jnp.concatenate([lifted_mid, skip_mid], axis=3)), weight_up_mid)
    )
    padded = faces_pad(jnp.concatenate([upsample(merged_mid, weight_lift_top), skip_top], axis=3))
    decoded = conv_valid(padded, weight_out).astype(jnp.bfloat16)
    return decoded.reshape(size_x, size_y, size_z * channels)


def solution(mesh):
    placed = (P("gx", "gy", "gz"), P(), P(), P(), P(), P(), P(), P(), P(), P())
    return jax.shard_map(
        body, mesh=mesh, in_specs=placed, out_specs=P("gx", "gy", "gz"), check_vma=False
    )
```

profile of v0, /device:TPU:1, one launch (start us, length us, event | category | flops | bytes accessed | tf_op | source)
XLA Modules:
  0.0 232.8 jit_solution(5235524929028799576)
XLA Ops:
  0.9 3.9 %collective-permute-start = (bf16[1,16,16,64]{3,2,1,0:T(8,128)(2,1)S(1)}, bf16[1,16,16,64]{3,2,1,0:T(8,128)(2,1)S(1)}, u32[]{:S(2)}, u32[]{:S(2)}) collective-permute-start(bf16[1,16,16,64]{3,2,1,0:T(8,128)(2,1)S(1)} %slice.579), channel_id=1, source_target_pairs={{0,64},{64,128},{128,192},{1,65},{65,129},{129,193},{2,66},{66,130... | collective-permute-start | bytes 98312 | tf_op jit(solution)/shard_map/ppermute | solution.py:15
  10.2 5.2 %collective-permute-start.2 = (bf16[10,1,16,64]{3,2,1,0:T(8,128)(2,1)S(1)}, bf16[10,1,16,64]{3,2,1,0:T(8,128)(2,1)S(1)}, u32[]{:S(2)}, u32[]{:S(2)}) collective-permute-start(bf16[10,1,16,64]{3,2,1,0:T(8,128)(2,1)S(1)} %get-tuple-element.76), channel_id=1, source_target_pairs={{0,8},{8,16},{16,24},{24,32},{32,40},{40,48},{48,56},{1,9},{9,17},... | collective-permute-start | bytes 61448 | tf_op jit(solution)/shard_map/ppermute | solution.py:15
  17.3 3.4 %collective-permute-done.3 = bf16[10,1,16,64]{3,2,1,0:T(8,128)(2,1)S(1)} collective-permute-done((bf16[10,1,16,64]{3,2,1,0:T(8,128)(2,1)S(1)}, bf16[10,1,16,64]{3,2,1,0:T(8,128)(2,1)S(1)}, u32[]{:S(2)}, u32[]{:S(2)}) %collective-permute-start.3) | collective-permute-done | bytes 20512 | tf_op jit(solution)/shard_map/ppermute | solution.py:17
  20.9 3.5 %collective-permute-start.4 = (bf16[10,18,1,64]{3,2,1,0:T(2,128)(2,1)S(1)}, bf16[10,18,1,64]{3,2,1,0:T(2,128)(2,1)S(1)}, u32[]{:S(2)}, u32[]{:S(2)}) collective-permute-start(bf16[10,18,1,64]{3,2,1,0:T(2,128)(2,1)S(1)} %get-tuple-element.74), channel_id=1, source_target_pairs={{0,1},{1,2},{2,3},{3,4},{4,5},{5,6},{6,7},{8,9},{9,10},{10,11},{11... | collective-permute-start | bytes 69128 | tf_op jit(solution)/shard_map/ppermute | solution.py:15
  26.0 3.9 %collective-permute-done.5 = bf16[10,18,1,64]{3,2,1,0:T(2,128)(2,1)S(1)} collective-permute-done((bf16[10,18,1,64]{3,2,1,0:T(2,128)(2,1)S(1)}, bf16[10,18,1,64]{3,2,1,0:T(2,128)(2,1)S(1)}, u32[]{:S(2)}, u32[]{:S(2)}) %collective-permute-start.5) | collective-permute-done | bytes 23072 | tf_op jit(solution)/shard_map/ppermute | solution.py:17
  45.5 4.9 %collective-permute-start.8 = (bf16[6,1,8,64]{3,2,1,0:T(8,128)(2,1)S(1)}, bf16[6,1,8,64]{3,2,1,0:T(8,128)(2,1)S(1)}, u32[]{:S(2)}, u32[]{:S(2)}) collective-permute-start(bf16[6,1,8,64]{3,2,1,0:T(8,128)(2,1)S(1)} %get-tuple-element.146), channel_id=1, source_target_pairs={{0,8},{8,16},{16,24},{24,32},{32,40},{40,48},{48,56},{1,9},{9,17},... | collective-permute-start | bytes 18440 | tf_op jit(solution)/shard_map/ppermute | solution.py:15
  55.5 3.5 %collective-permute-start.10 = (bf16[6,10,1,64]{3,2,1,0:T(2,128)(2,1)S(1)}, bf16[6,10,1,64]{3,2,1,0:T(2,128)(2,1)S(1)}, u32[]{:S(2)}, u32[]{:S(2)}) collective-permute-start(bf16[6,10,1,64]{3,2,1,0:T(2,128)(2,1)S(1)} %get-tuple-element.142), channel_id=1, source_target_pairs={{0,1},{1,2},{2,3},{3,4},{4,5},{5,6},{6,7},{8,9},{9,10},{10,11},{11... | collective-permute-start | bytes 23048 | tf_op jit(solution)/shard_map/ppermute | solution.py:15
  60.4 4.5 %collective-permute-done.11 = bf16[6,10,1,64]{3,2,1,0:T(2,128)(2,1)S(1)} collective-permute-done((bf16[6,10,1,64]{3,2,1,0:T(2,128)(2,1)S(1)}, bf16[6,10,1,64]{3,2,1,0:T(2,128)(2,1)S(1)}, u32[]{:S(2)}, u32[]{:S(2)}) %collective-permute-start.11) | collective-permute-done | bytes 7712 | tf_op jit(solution)/shard_map/ppermute | solution.py:17
  71.0 3.5 %collective-permute-done.13 = bf16[1,8,8,128]{3,2,1,0:T(8,128)(2,1)S(1)} collective-permute-done((bf16[1,8,8,128]{3,2,1,0:T(8,128)(2,1)S(1)}, bf16[1,8,8,128]{3,2,1,0:T(8,128)(2,1)S(1)}, u32[]{:S(2)}, u32[]{:S(2)}) %collective-permute-start.13) | collective-permute-done | bytes 16416 | tf_op jit(solution)/shard_map/ppermute | solution.py:17
  74.5 4.1 %collective-permute-start.14 = (bf16[6,1,8,128]{3,2,1,0:T(8,128)(2,1)S(1)}, bf16[6,1,8,128]{3,2,1,0:T(8,128)(2,1)S(1)}, u32[]{:S(2)}, u32[]{:S(2)}) collective-permute-start(bf16[6,1,8,128]{3,2,1,0:T(8,128)(2,1)S(1)} %get-tuple-element.144), channel_id=1, source_target_pairs={{0,8},{8,16},{16,24},{24,32},{32,40},{40,48},{48,56},{1,9},{9,17},... | collective-permute-start | bytes 36872 | tf_op jit(solution)/shard_map/ppermute | solution.py:15
  83.8 5.2 %collective-permute-start.16 = (bf16[6,10,1,128]{3,2,1,0:T(2,128)(2,1)S(1)}, bf16[6,10,1,128]{3,2,1,0:T(2,128)(2,1)S(1)}, u32[]{:S(2)}, u32[]{:S(2)}) collective-permute-start(bf16[6,10,1,128]{3,2,1,0:T(2,128)(2,1)S(1)} %get-tuple-element.140), channel_id=1, source_target_pairs={{0,1},{1,2},{2,3},{3,4},{4,5},{5,6},{6,7},{8,9},{9,10},{10,11},{11... | collective-permute-start | bytes 46088 | tf_op jit(solution)/shard_map/ppermute | solution.py:15
  90.4 3.5 %collective-permute-done.17 = bf16[6,10,1,128]{3,2,1,0:T(2,128)(2,1)S(1)} collective-permute-done((bf16[6,10,1,128]{3,2,1,0:T(2,128)(2,1)S(1)}, bf16[6,10,1,128]{3,2,1,0:T(2,128)(2,1)S(1)}, u32[]{:S(2)}, u32[]{:S(2)}) %collective-permute-start.17) | collective-permute-done | bytes 15392 | tf_op jit(solution)/shard_map/ppermute | solution.py:17
  102.4 4.3 %collective-permute-start.20 = (bf16[4,1,4,128]{3,2,1,0:T(4,128)(2,1)S(1)}, bf16[4,1,4,128]{3,2,1,0:T(4,128)(2,1)S(1)}, u32[]{:S(2)}, u32[]{:S(2)}) collective-permute-start(bf16[4,1,4,128]{3,2,1,0:T(4,128)(2,1)S(1)} %get-tuple-element.169), channel_id=1, source_target_pairs={{0,8},{8,16},{16,24},{24,32},{32,40},{40,48},{48,56},{1,9},{9,17},... | collective-permute-start | bytes 12296 | tf_op jit(solution)/shard_map/ppermute | solution.py:15
  111.7 3.6 %collective-permute-start.22 = (bf16[4,6,1,128]{3,2,1,0:T(2,128)(2,1)S(1)}, bf16[4,6,1,128]{3,2,1,0:T(2,128)(2,1)S(1)}, u32[]{:S(2)}, u32[]{:S(2)}) collective-permute-start(bf16[4,6,1,128]{3,2,1,0:T(2,128)(2,1)S(1)} %get-tuple-element.165), channel_id=1, source_target_pairs={{0,1},{1,2},{2,3},{3,4},{4,5},{5,6},{6,7},{8,9},{9,10},{10,11},{11... | collective-permute-start | bytes 18440 | tf_op jit(solution)/shard_map/ppermute | solution.py:15
  129.5 4.8 %collective-permute-start.26 = (bf16[4,1,4,256]{3,2,1,0:T(4,128)(2,1)S(1)}, bf16[4,1,4,256]{3,2,1,0:T(4,128)(2,1)S(1)}, u32[]{:S(2)}, u32[]{:S(2)}) collective-permute-start(bf16[4,1,4,256]{3,2,1,0:T(4,128)(2,1)S(1)} %get-tuple-element.163), channel_id=1, source_target_pairs={{0,8},{8,16},{16,24},{24,32},{32,40},{40,48},{48,56},{1,9},{9,17},... | collective-permute-start | bytes 24584 | tf_op jit(solution)/shard_map/ppermute | solution.py:15
  165.5 3.3 %collective-permute-done.31 = bf16[1,8,8,256]{3,2,1,0:T(8,128)(2,1)S(1)} collective-permute-done((bf16[1,8,8,256]{3,2,1,0:T(8,128)(2,1)S(1)}, bf16[1,8,8,256]{3,2,1,0:T(8,128)(2,1)S(1)}, u32[]{:S(2)}, u32[]{:S(2)}) %collective-permute-start.31) | collective-permute-done | bytes 32800 | tf_op jit(solution)/shard_map/ppermute | solution.py:17
  168.9 3.7 %collective-permute-start.32 = (bf16[6,1,8,256]{3,2,1,0:T(8,128)(2,1)S(1)}, bf16[6,1,8,256]{3,2,1,0:T(8,128)(2,1)S(1)}, u32[]{:S(2)}, u32[]{:S(2)}) collective-permute-start(bf16[6,1,8,256]{3,2,1,0:T(8,128)(2,1)S(1)} %get-tuple-element.127), channel_id=1, source_target_pairs={{0,8},{8,16},{16,24},{24,32},{32,40},{40,48},{48,56},{1,9},{9,17},... | collective-permute-start | bytes 73736 | tf_op jit(solution)/shard_map/ppermute | solution.py:15
  177.8 4.5 %collective-permute-start.34 = (bf16[6,10,1,256]{3,2,1,0:T(2,128)(2,1)S(1)}, bf16[6,10,1,256]{3,2,1,0:T(2,128)(2,1)S(1)}, u32[]{:S(2)}, u32[]{:S(2)}) collective-permute-start(bf16[6,10,1,256]{3,2,1,0:T(2,128)(2,1)S(1)} %get-tuple-element.116), channel_id=1, source_target_pairs={{0,1},{1,2},{2,3},{3,4},{4,5},{5,6},{6,7},{8,9},{9,10},{10,11},{11... | collective-permute-start | bytes 92168 | tf_op jit(solution)/shard_map/ppermute | solution.py:15
  183.8 3.5 %collective-permute-done.35 = bf16[6,10,1,256]{3,2,1,0:T(2,128)(2,1)S(1)} collective-permute-done((bf16[6,10,1,256]{3,2,1,0:T(2,128)(2,1)S(1)}, bf16[6,10,1,256]{3,2,1,0:T(2,128)(2,1)S(1)}, u32[]{:S(2)}, u32[]{:S(2)}) %collective-permute-start.35) | collective-permute-done | bytes 30752 | tf_op jit(solution)/shard_map/ppermute | solution.py:17
  195.3 4.1 %collective-permute-done.37 = bf16[1,16,16,128]{3,2,1,0:T(8,128)(2,1)S(1)} collective-permute-done((bf16[1,16,16,128]{3,2,1,0:T(8,128)(2,1)S(1)}, bf16[1,16,16,128]{3,2,1,0:T(8,128)(2,1)S(1)}, u32[]{:S(2)}, u32[]{:S(2)}) %collective-permute-start.37) | collective-permute-done | bytes 65568 | tf_op jit(solution)/shard_map/ppermute | solution.py:17
  199.5 4.0 %collective-permute-start.38 = (bf16[10,1,16,128]{3,2,1,0:T(8,128)(2,1)S(1)}, bf16[10,1,16,128]{3,2,1,0:T(8,128)(2,1)S(1)}, u32[]{:S(2)}, u32[]{:S(2)}) collective-permute-start(bf16[10,1,16,128]{3,2,1,0:T(8,128)(2,1)S(1)} %get-tuple-element.52), channel_id=1, source_target_pairs={{0,8},{8,16},{16,24},{24,32},{32,40},{40,48},{48,56},{1,9},{9,17},... | collective-permute-start | bytes 122888 | tf_op jit(solution)/shard_map/ppermute | solution.py:15
  205.4 3.4 %collective-permute-done.39 = bf16[10,1,16,128]{3,2,1,0:T(8,128)(2,1)S(1)} collective-permute-done((bf16[10,1,16,128]{3,2,1,0:T(8,128)(2,1)S(1)}, bf16[10,1,16,128]{3,2,1,0:T(8,128)(2,1)S(1)}, u32[]{:S(2)}, u32[]{:S(2)}) %collective-permute-start.39) | collective-permute-done | bytes 40992 | tf_op jit(solution)/shard_map/ppermute | solution.py:17
  213.9 3.5 %collective-permute-done.41 = bf16[10,18,1,128]{3,2,1,0:T(2,128)(2,1)S(1)} collective-permute-done((bf16[10,18,1,128]{3,2,1,0:T(2,128)(2,1)S(1)}, bf16[10,18,1,128]{3,2,1,0:T(2,128)(2,1)S(1)}, u32[]{:S(2)}, u32[]{:S(2)}) %collective-permute-start.41) | collective-permute-done | bytes 46112 | tf_op jit(solution)/shard_map/ppermute | solution.py:17
  217.4 6.0 %fusion.3 = bf16[10,18,16,384]{3,2,1,0:T(8,128)(2,1)S(1)} fusion(bf16[10,18,1,128]{3,2,1,0:T(2,128)(2,1)S(1)} %collective-permute-done.41, bf16[10,1,16,128]{3,2,1,0:T(8,128)(2,1)S(1)} %collective-permute-done.39, bf16[10,1,16,128]{3,2,1,0:T(8,128)(2,1)S(1)} %collective-permute-done.38, bf16[1,16,16,128]{3,2,1,0:T(8,128)(2,1)S(1)} %collective-permute-done.37, ...), kind=kLoop, calls=%fused_computation.20 | loop fusion | flops 44236800 | bytes 3041280 | tf_op jit(solution)/shard_map/concatenate | solution.py:34
  (240 shorter events, 133.3 us)
Async XLA Ops:
  0.9 6.9 %collective-permute-start = (bf16[1,16,16,64]{3,2,1,0:T(8,128)(2,1)S(1)}, bf16[1,16,16,64]{3,2,1,0:T(8,128)(2,1)S(1)}, u32[]{:S(2)}, u32[]{:S(2)}) collective-permute-start(bf16[1,16,16,64]{3,2,1,0:T(8,128)(2,1)S(1)} %slice.579), channel_id=1, source_target_pairs={{0,64},{64,128},{128,192},{1,65},{65,129},{129,193},{2,66},{66,130... | collective-permute-start | bytes 98312 | tf_op jit(solution)/shard_map/ppermute | solution.py:15
  5.0 5.1 %collective-permute-start.1 = (bf16[1,16,16,64]{3,2,1,0:T(8,128)(2,1)S(1)}, bf16[1,16,16,64]{3,2,1,0:T(8,128)(2,1)S(1)}, u32[]{:S(2)}, u32[]{:S(2)}) collective-permute-start(bf16[1,16,16,64]{3,2,1,0:T(8,128)(2,1)S(1)} %slice.581), channel_id=1, source_target_pairs={{64,0},{128,64},{192,128},{65,1},{129,65},{193,129},{66,2},{130,66... | collective-permute-start | bytes 98312 | tf_op jit(solution)/shard_map/ppermute | solution.py:17
  10.2 7.1 %collective-permute-start.2 = (bf16[10,1,16,64]{3,2,1,0:T(8,128)(2,1)S(1)}, bf16[10,1,16,64]{3,2,1,0:T(8,128)(2,1)S(1)}, u32[]{:S(2)}, u32[]{:S(2)}) collective-permute-start(bf16[10,1,16,64]{3,2,1,0:T(8,128)(2,1)S(1)} %get-tuple-element.76), channel_id=1, source_target_pairs={{0,8},{8,16},{16,24},{24,32},{32,40},{40,48},{48,56},{1,9},{9,17},... | collective-permute-start | bytes 61448 | tf_op jit(solution)/shard_map/ppermute | solution.py:15
  15.4 5.3 %collective-permute-start.3 = (bf16[10,1,16,64]{3,2,1,0:T(8,128)(2,1)S(1)}, bf16[10,1,16,64]{3,2,1,0:T(8,128)(2,1)S(1)}, u32[]{:S(2)}, u32[]{:S(2)}) collective-permute-start(bf16[10,1,16,64]{3,2,1,0:T(8,128)(2,1)S(1)} %get-tuple-element.77), channel_id=1, source_target_pairs={{8,0},{16,8},{24,16},{32,24},{40,32},{48,40},{56,48},{9,1},{17,9},... | collective-permute-start | bytes 61448 | tf_op jit(solution)/shard_map/ppermute | solution.py:17
  20.9 5.1 %collective-permute-start.4 = (bf16[10,18,1,64]{3,2,1,0:T(2,128)(2,1)S(1)}, bf16[10,18,1,64]{3,2,1,0:T(2,128)(2,1)S(1)}, u32[]{:S(2)}, u32[]{:S(2)}) collective-permute-start(bf16[10,18,1,64]{3,2,1,0:T(2,128)(2,1)S(1)} %get-tuple-element.74), channel_id=1, source_target_pairs={{0,1},{1,2},{2,3},{3,4},{4,5},{5,6},{6,7},{8,9},{9,10},{10,11},{11... | collective-permute-start | bytes 69128 | tf_op jit(solution)/shard_map/ppermute | solution.py:15
  24.5 5.5 %collective-permute-start.5 = (bf16[10,18,1,64]{3,2,1,0:T(2,128)(2,1)S(1)}, bf16[10,18,1,64]{3,2,1,0:T(2,128)(2,1)S(1)}, u32[]{:S(2)}, u32[]{:S(2)}) collective-permute-start(bf16[10,18,1,64]{3,2,1,0:T(2,128)(2,1)S(1)} %get-tuple-element.75), channel_id=1, source_target_pairs={{1,0},{2,1},{3,2},{4,3},{5,4},{6,5},{7,6},{9,8},{10,9},{11,10},{12... | collective-permute-start | bytes 69128 | tf_op jit(solution)/shard_map/ppermute | solution.py:17
  45.5 6.8 %collective-permute-start.8 = (bf16[6,1,8,64]{3,2,1,0:T(8,128)(2,1)S(1)}, bf16[6,1,8,64]{3,2,1,0:T(8,128)(2,1)S(1)}, u32[]{:S(2)}, u32[]{:S(2)}) collective-permute-start(bf16[6,1,8,64]{3,2,1,0:T(8,128)(2,1)S(1)} %get-tuple-element.146), channel_id=1, source_target_pairs={{0,8},{8,16},{16,24},{24,32},{32,40},{40,48},{48,56},{1,9},{9,17},... | collective-permute-start | bytes 18440 | tf_op jit(solution)/shard_map/ppermute | solution.py:15
  50.4 5.0 %collective-permute-start.9 = (bf16[6,1,8,64]{3,2,1,0:T(8,128)(2,1)S(1)}, bf16[6,1,8,64]{3,2,1,0:T(8,128)(2,1)S(1)}, u32[]{:S(2)}, u32[]{:S(2)}) collective-permute-start(bf16[6,1,8,64]{3,2,1,0:T(8,128)(2,1)S(1)} %get-tuple-element.147), channel_id=1, source_target_pairs={{8,0},{16,8},{24,16},{32,24},{40,32},{48,40},{56,48},{9,1},{17,9},... | collective-permute-start | bytes 18440 | tf_op jit(solution)/shard_map/ppermute | solution.py:17
  59.0 5.8 %collective-permute-start.11 = (bf16[6,10,1,64]{3,2,1,0:T(2,128)(2,1)S(1)}, bf16[6,10,1,64]{3,2,1,0:T(2,128)(2,1)S(1)}, u32[]{:S(2)}, u32[]{:S(2)}) collective-permute-start(bf16[6,10,1,64]{3,2,1,0:T(2,128)(2,1)S(1)} %get-tuple-element.143), channel_id=1, source_target_pairs={{1,0},{2,1},{3,2},{4,3},{5,4},{6,5},{7,6},{9,8},{10,9},{11,10},{12... | collective-permute-start | bytes 23048 | tf_op jit(solution)/shard_map/ppermute | solution.py:17
  74.5 6.1 %collective-permute-start.14 = (bf16[6,1,8,128]{3,2,1,0:T(8,128)(2,1)S(1)}, bf16[6,1,8,128]{3,2,1,0:T(8,128)(2,1)S(1)}, u32[]{:S(2)}, u32[]{:S(2)}) collective-permute-start(bf16[6,1,8,128]{3,2,1,0:T(8,128)(2,1)S(1)} %get-tuple-element.144), channel_id=1, source_target_pairs={{0,8},{8,16},{16,24},{24,32},{32,40},{40,48},{48,56},{1,9},{9,17},... | collective-permute-start | bytes 36872 | tf_op jit(solution)/shard_map/ppermute | solution.py:15
  78.7 5.0 %collective-permute-start.15 = (bf16[6,1,8,128]{3,2,1,0:T(8,128)(2,1)S(1)}, bf16[6,1,8,128]{3,2,1,0:T(8,128)(2,1)S(1)}, u32[]{:S(2)}, u32[]{:S(2)}) collective-permute-start(bf16[6,1,8,128]{3,2,1,0:T(8,128)(2,1)S(1)} %get-tuple-element.145), channel_id=1, source_target_pairs={{8,0},{16,8},{24,16},{32,24},{40,32},{48,40},{56,48},{9,1},{17,9},... | collective-permute-start | bytes 36872 | tf_op jit(solution)/shard_map/ppermute | solution.py:17
  83.8 6.6 %collective-permute-start.16 = (bf16[6,10,1,128]{3,2,1,0:T(2,128)(2,1)S(1)}, bf16[6,10,1,128]{3,2,1,0:T(2,128)(2,1)S(1)}, u32[]{:S(2)}, u32[]{:S(2)}) collective-permute-start(bf16[6,10,1,128]{3,2,1,0:T(2,128)(2,1)S(1)} %get-tuple-element.140), channel_id=1, source_target_pairs={{0,1},{1,2},{2,3},{3,4},{4,5},{5,6},{6,7},{8,9},{9,10},{10,11},{11... | collective-permute-start | bytes 46088 | tf_op jit(solution)/shard_map/ppermute | solution.py:15
  102.4 6.2 %collective-permute-start.20 = (bf16[4,1,4,128]{3,2,1,0:T(4,128)(2,1)S(1)}, bf16[4,1,4,128]{3,2,1,0:T(4,128)(2,1)S(1)}, u32[]{:S(2)}, u32[]{:S(2)}) collective-permute-start(bf16[4,1,4,128]{3,2,1,0:T(4,128)(2,1)S(1)} %get-tuple-element.169), channel_id=1, source_target_pairs={{0,8},{8,16},{16,24},{24,32},{32,40},{40,48},{48,56},{1,9},{9,17},... | collective-permute-start | bytes 12296 | tf_op jit(solution)/shard_map/ppermute | solution.py:15
  111.7 5.9 %collective-permute-start.22 = (bf16[4,6,1,128]{3,2,1,0:T(2,128)(2,1)S(1)}, bf16[4,6,1,128]{3,2,1,0:T(2,128)(2,1)S(1)}, u32[]{:S(2)}, u32[]{:S(2)}) collective-permute-start(bf16[4,6,1,128]{3,2,1,0:T(2,128)(2,1)S(1)} %get-tuple-element.165), channel_id=1, source_target_pairs={{0,1},{1,2},{2,3},{3,4},{4,5},{5,6},{6,7},{8,9},{9,10},{10,11},{11... | collective-permute-start | bytes 18440 | tf_op jit(solution)/shard_map/ppermute | solution.py:15
  129.5 6.7 %collective-permute-start.26 = (bf16[4,1,4,256]{3,2,1,0:T(4,128)(2,1)S(1)}, bf16[4,1,4,256]{3,2,1,0:T(4,128)(2,1)S(1)}, u32[]{:S(2)}, u32[]{:S(2)}) collective-permute-start(bf16[4,1,4,256]{3,2,1,0:T(4,128)(2,1)S(1)} %get-tuple-element.163), channel_id=1, source_target_pairs={{0,8},{8,16},{16,24},{24,32},{32,40},{40,48},{48,56},{1,9},{9,17},... | collective-permute-start | bytes 24584 | tf_op jit(solution)/shard_map/ppermute | solution.py:15
  139.4 9.0 %collective-permute-start.28 = (bf16[4,6,1,256]{3,2,1,0:T(2,128)(2,1)S(1)}, bf16[4,6,1,256]{3,2,1,0:T(2,128)(2,1)S(1)}, u32[]{:S(2)}, u32[]{:S(2)}) collective-permute-start(bf16[4,6,1,256]{3,2,1,0:T(2,128)(2,1)S(1)} %get-tuple-element.161), channel_id=1, source_target_pairs={{0,1},{1,2},{2,3},{3,4},{4,5},{5,6},{6,7},{8,9},{9,10},{10,11},{11... | collective-permute-start | bytes 36872 | tf_op jit(solution)/shard_map/ppermute | solution.py:15
  142.2 6.2 %collective-permute-start.29 = (bf16[4,6,1,256]{3,2,1,0:T(2,128)(2,1)S(1)}, bf16[4,6,1,256]{3,2,1,0:T(2,128)(2,1)S(1)}, u32[]{:S(2)}, u32[]{:S(2)}) collective-permute-start(bf16[4,6,1,256]{3,2,1,0:T(2,128)(2,1)S(1)} %get-tuple-element.162), channel_id=1, source_target_pairs={{1,0},{2,1},{3,2},{4,3},{5,4},{6,5},{7,6},{9,8},{10,9},{11,10},{12... | collective-permute-start | bytes 36872 | tf_op jit(solution)/shard_map/ppermute | solution.py:17
  168.9 5.6 %collective-permute-start.32 = (bf16[6,1,8,256]{3,2,1,0:T(8,128)(2,1)S(1)}, bf16[6,1,8,256]{3,2,1,0:T(8,128)(2,1)S(1)}, u32[]{:S(2)}, u32[]{:S(2)}) collective-permute-start(bf16[6,1,8,256]{3,2,1,0:T(8,128)(2,1)S(1)} %get-tuple-element.127), channel_id=1, source_target_pairs={{0,8},{8,16},{16,24},{24,32},{32,40},{40,48},{48,56},{1,9},{9,17},... | collective-permute-start | bytes 73736 | tf_op jit(solution)/shard_map/ppermute | solution.py:15
  172.5 5.1 %collective-permute-start.33 = (bf16[6,1,8,256]{3,2,1,0:T(8,128)(2,1)S(1)}, bf16[6,1,8,256]{3,2,1,0:T(8,128)(2,1)S(1)}, u32[]{:S(2)}, u32[]{:S(2)}) collective-permute-start(bf16[6,1,8,256]{3,2,1,0:T(8,128)(2,1)S(1)} %get-tuple-element.128), channel_id=1, source_target_pairs={{8,0},{16,8},{24,16},{32,24},{40,32},{48,40},{56,48},{9,1},{17,9},... | collective-permute-start | bytes 73736 | tf_op jit(solution)/shard_map/ppermute | solution.py:17
  177.8 6.1 %collective-permute-start.34 = (bf16[6,10,1,256]{3,2,1,0:T(2,128)(2,1)S(1)}, bf16[6,10,1,256]{3,2,1,0:T(2,128)(2,1)S(1)}, u32[]{:S(2)}, u32[]{:S(2)}) collective-permute-start(bf16[6,10,1,256]{3,2,1,0:T(2,128)(2,1)S(1)} %get-tuple-element.116), channel_id=1, source_target_pairs={{0,1},{1,2},{2,3},{3,4},{4,5},{5,6},{6,7},{8,9},{9,10},{10,11},{11... | collective-permute-start | bytes 92168 | tf_op jit(solution)/shard_map/ppermute | solution.py:15
  193.5 5.9 %collective-permute-start.37 = (bf16[1,16,16,128]{3,2,1,0:T(8,128)(2,1)S(1)}, bf16[1,16,16,128]{3,2,1,0:T(8,128)(2,1)S(1)}, u32[]{:S(2)}, u32[]{:S(2)}) collective-permute-start(bf16[1,16,16,128]{3,2,1,0:T(8,128)(2,1)S(1)} %get-tuple-element.55), channel_id=1, source_target_pairs={{64,0},{128,64},{192,128},{65,1},{129,65},{193,129},{66,2},{130,66... | collective-permute-start | bytes 196616 | tf_op jit(solution)/shard_map/ppermute | solution.py:17
  199.5 5.9 %collective-permute-start.38 = (bf16[10,1,16,128]{3,2,1,0:T(8,128)(2,1)S(1)}, bf16[10,1,16,128]{3,2,1,0:T(8,128)(2,1)S(1)}, u32[]{:S(2)}, u32[]{:S(2)}) collective-permute-start(bf16[10,1,16,128]{3,2,1,0:T(8,128)(2,1)S(1)} %get-tuple-element.52), channel_id=1, source_target_pairs={{0,8},{8,16},{16,24},{24,32},{32,40},{40,48},{48,56},{1,9},{9,17},... | collective-permute-start | bytes 122888 | tf_op jit(solution)/shard_map/ppermute | solution.py:15
  203.5 5.3 %collective-permute-start.39 = (bf16[10,1,16,128]{3,2,1,0:T(8,128)(2,1)S(1)}, bf16[10,1,16,128]{3,2,1,0:T(8,128)(2,1)S(1)}, u32[]{:S(2)}, u32[]{:S(2)}) collective-permute-start(bf16[10,1,16,128]{3,2,1,0:T(8,128)(2,1)S(1)} %get-tuple-element.53), channel_id=1, source_target_pairs={{8,0},{16,8},{24,16},{32,24},{40,32},{48,40},{56,48},{9,1},{17,9},... | collective-permute-start | bytes 122888 | tf_op jit(solution)/shard_map/ppermute | solution.py:17
  212.1 5.3 %collective-permute-start.41 = (bf16[10,18,1,128]{3,2,1,0:T(2,128)(2,1)S(1)}, bf16[10,18,1,128]{3,2,1,0:T(2,128)(2,1)S(1)}, u32[]{:S(2)}, u32[]{:S(2)}) collective-permute-start(bf16[10,18,1,128]{3,2,1,0:T(2,128)(2,1)S(1)} %get-tuple-element.51), channel_id=1, source_target_pairs={{1,0},{2,1},{3,2},{4,3},{5,4},{6,5},{7,6},{9,8},{10,9},{11,10},{12... | collective-permute-start | bytes 138248 | tf_op jit(solution)/shard_map/ppermute | solution.py:17
  (30 other events, 426.2 us)
where the time goes:
time: 235 us; the launch traced here: 233 us
  starting transfers between devices  105 us (45%)
  waiting for transfers between devices  66.7 us (28%)
  matrix products  25.1 us (11%)
  local copies, waits for them, and re-layouts  22.7 us (10%)
  other arithmetic  11.4 us (5%)
    ppermute x21, starting transfers between devices, padded_2(): lax.ppermute(tail, axis, [(i, (i + 1) % count) for i in range(ends)])  73.4 us
    ppermute x21, waiting for transfers between devices, padded_2(): lax.ppermute(head, axis, [((i + 1) % count, i) for i in range(ends)])  66 us
    ppermute x21, starting transfers between devices, padded_2(): lax.ppermute(head, axis, [((i + 1) % count, i) for i in range(ends)])  31.8 us
    dot_general x61, matrix products, conv_valid(): total = total + jnp.dot(piece, kernel, preferred_element_type=jnp.float32)  24.2 us
    concatenate x7, other arithmetic, conv_valid(): jnp.concatenate([padded[:, :, depth:depth + size_z, :] for depth in range...  9.4 us
    reshape x18, local copies, waits for them, and re-layouts, conv_valid(): stacked[shift_x:shift_x + size_x, shift_y:shift_y + size_y]  6.37 us
    slice x16, local copies, waits for them, and re-layouts, conv_valid(): kernel = weight[shift_x, shift_y].reshape(3 * inputs, outputs)  5 us
    slice x7, local copies, waits for them, and re-layouts, conv_valid(): stacked[shift_x:shift_x + size_x, shift_y:shift_y + size_y]  4.89 us
  transfers between devices with their start and end apart: 42, of which 22 were waited for; matrix products, arithmetic and copies ran while one was open for 3% of the time, Pallas kernels for 0%

commit v1 on v0

v1 whole, which is shorter than its diff:
```python
import functools

import jax
import jax.numpy as jnp
from jax import lax
from jax.experimental import pallas as pl
from jax.experimental.pallas import tpu as pltpu
from jax.sharding import PartitionSpec as P

F32 = jnp.float32
BF16 = jnp.bfloat16
MESH = pl.DeviceIdType.MESH

DIRS = [
    (dx, dy, dz)
    for dx in (0, -1, 1)
    for dz in (0, -1, 1)
    for dy in (0, -1, 1)
    if (dx, dy, dz) != (0, 0, 0)
]
LOW_DIRS = [
    (dx, dy, dz)
    for dx in (0, -1, 1, -2, 2)
    for dz in (0, -1, 1)
    for dy in (0, -1, 1)
    if (dx, dy, dz) != (0, 0, 0)
]


def dot(a, b):
    return jnp.dot(a, b, preferred_element_type=F32)


def side(step):
    return 0 if step == 1 else 1


SCRATCH = dict(
    k_top=((1728, 64), BF16),
    k_da=((1728, 128), BF16),
    k_db=((3456, 128), BF16),
    k_la=((3456, 256), BF16),
    k_lb=((6912, 256), BF16),
    k_ll=((256, 1024), BF16),
    k_um=((6912, 128), BF16),
    k_lt=((128, 512), BF16),
    k_out=((3456, 64), BF16),
    t_top=((9, 512, 256), BF16),
    t_skip=((9, 512, 256), BF16),
    t_lift=((9, 512, 256), BF16),
    t_da=((9, 256, 256), BF16),
    t_lt=((256, 256), BF16),
    wide=((10, 320, 128), F32),
    vol0=((10, 16, 1280), BF16),
    vol1=((10, 16, 1280), BF16),
    vol2=((10, 16, 1280), BF16),
    skip0=((10, 16, 1280), BF16),
    skip1=((10, 16, 1280), BF16),
    skip2=((10, 16, 1280), BF16),
    lift0=((10, 16, 1280), BF16),
    lift1=((10, 16, 1280), BF16),
    lift2=((10, 16, 1280), BF16),
    vol_a=((2, 4, 16, 128), BF16),
    vol_b=((2, 2, 16, 128), BF16),
    vol_r=((2, 12, 16, 128), BF16),
    skip_a=((2, 4, 16, 128), BF16),
    skip_b=((2, 2, 16, 128), BF16),
    skip_r=((2, 12, 16, 128), BF16),
    tmp=((4, 16, 128), F32),
    top_out=((8, 128, 128), F32),
    part=((4, 128, 256), F32),
    pm=((4, 6, 16, 128), BF16),
    pm_y=((2, 2, 16, 128), BF16),
    pm_r=((2, 3, 3, 2, 16, 128), BF16),
    pm_t=((2, 2, 16, 128), F32),
    pm_wide=((8, 24, 768), F32),
    pm_s=((3, 8, 16, 768), BF16),
    fm_wide=((6, 10, 24, 128), F32),
    fm_s=((6, 64, 1152), BF16),
    sm_out=((4, 8, 8, 128), F32),
    sm=((8, 6, 16, 128), BF16),
    sm_y=((2, 4, 16, 128), BF16),
    sm_r=((2, 3, 3, 4, 16, 128), BF16),
    sm_t=((4, 16, 128), F32),
    pl_t=((2, 4, 8, 128), F32),
    pl_f=((2, 16, 128), F32),
    pl_r=((5, 3, 3, 2, 16, 128), BF16),
    pl_g=((3, 16, 128), F32),
    pl_wide=((8, 10, 16, 128), F32),
    pl_s=((8, 64, 1152), BF16),
    fl_wide=((6, 8, 16, 256), F32),
    fl_s=((6, 48, 2304), BF16),
    jm_wide=((2, 8, 12, 24, 128), F32),
    jm_s=((3, 8, 12, 16, 256), BF16),
    mg_wide=((2, 6, 10, 32, 128), F32),
)
NAMES = list(SCRATCH)
WEIGHTS = ("k_top", "k_da", "k_db", "k_la", "k_lb", "k_ll", "k_um", "k_lt", "k_out")


class Exchange:
    def __init__(self, dirs, message, send, recv, here, sizes):
        self.dirs, self.message = dirs, message
        self.send, self.recv = send, recv
        self.here, self.sizes = here, sizes

    def inside(self, step, sign):
        ok = None
        for at, size, s in zip(self.here, self.sizes, step):
            s = s * sign
            if s == 0:
                continue
            this = at + s < size if s > 0 else at + s >= 0
            ok = this if ok is None else jnp.logical_and(ok, this)
        return ok

    def copy(self, i):
        step = self.dirs[i]
        src, dst = self.message(step)
        there = tuple(at + s for at, s in zip(self.here, step))
        return pltpu.make_async_remote_copy(
            src_ref=src,
            dst_ref=dst,
            send_sem=self.send.at[i],
            recv_sem=self.recv.at[i],
            device_id=there,
            device_id_type=MESH,
        )

    def start(self):
        for i, step in enumerate(self.dirs):
            pl.when(self.inside(step, 1))(lambda i=i: self.copy(i).start())

    def wait_recv(self):
        for i, step in enumerate(self.dirs):
            pl.when(self.inside(step, -1))(lambda i=i: self.copy(i).wait_recv())

    def wait_send(self):
        for i, step in enumerate(self.dirs):
            pl.when(self.inside(step, 1))(lambda i=i: self.copy(i).wait_send())


def kernel(sizes, *refs):
    vol, weights, out = refs[0], refs[1:10], refs[10]
    n = len(NAMES)
    b = dict(zip(NAMES, refs[11 : 11 + n]))
    (load_sem, vol_ss, vol_rs, skip_ss, skip_rs, pm_ss, pm_rs, sm_ss, sm_rs, pl_ss, pl_rs) = refs[11 + n :]
    here = tuple(lax.axis_index(name) for name in ("gx", "gy", "gz"))
    gx, gy, gz = here
    tile = lambda t: slice(128 * t, 128 * t + 128)

    vol1 = b["vol1"]
    vol_load = pltpu.make_async_copy(vol, vol1.at[1:9, :, 128:1152], load_sem.at[9])
    vol_load.start()
    loads = {}
    for i, name in enumerate(WEIGHTS):
        loads[name] = pltpu.make_async_copy(weights[i], b[name], load_sem.at[i])
        loads[name].start()

    def zero(ref, *at):
        if at:
            ref[at] = jnp.zeros(ref.at[at].shape, ref.dtype)
        else:
            ref[...] = jnp.zeros(ref.shape, ref.dtype)

    everything = slice(None)
    for name in ("vol1", "skip1"):
        zero(b[name], slice(0, 1))
        zero(b[name], slice(9, 10))
        zero(b[name], slice(1, 9), everything, tile(0))
        zero(b[name], slice(1, 9), everything, tile(9))
    for name in ("vol_r", "skip_r", "pm_r", "sm_r", "pl_r"):
        zero(b[name])
    for name, width, lo, hi in (("pm", 4, 1, 3), ("sm", 8, 2, 6)):
        zero(b[name], slice(0, lo))
        zero(b[name], slice(hi, width))
        zero(b[name], slice(lo, hi), slice(0, 1))
        zero(b[name], slice(lo, hi), slice(5, 6))

    barrier = pltpu.get_barrier_semaphore()
    low_x = Exchange(LOW_DIRS, None, None, None, here, sizes)
    for step in LOW_DIRS:

        @pl.when(low_x.inside(step, 1))
        def _(step=step):
            pl.semaphore_signal(
                barrier,
                inc=1,
                device_id=tuple(at + s for at, s in zip(here, step)),
                device_id_type=MESH,
            )

    def reach(at, size, far):
        count = jnp.int32(1)
        for s in range(1, far + 1):
            count = count + jnp.where(at >= s, 1, 0) + jnp.where(at + s < size, 1, 0)
        return count

    greeted = reach(gx, sizes[0], 2) * reach(gy, sizes[1], 1) * reach(gz, sizes[2], 1) - 1

    wide = b["wide"]
    tmp = b["tmp"]

    def stage_top(cells, a, bb):
        for x in range(1, 9):
            for t in range(1, 9):
                wide[t, 32 * x + 8 : 32 * x + 24, :] = cells[x, :, tile(t)].astype(F32)
        for s, y in ((0, 15), (1, 0)):
            for tp in range(4):
                pair = [
                    wide[2 * tp + h + 1, pl.ds(32 + 8 + y, 8, stride=32), :] for h in range(2)
                ]
                a[s, tp] = jnp.concatenate(pair, axis=0).astype(BF16)
            for xs, x in ((0, 8), (1, 1)):
                for t in range(8):
                    tmp[2 * s + xs, t : t + 1, :] = wide[t + 1, 32 * x + 8 + y : 32 * x + 9 + y, :]
                for t in range(8, 16):
                    tmp[2 * s + xs, t : t + 1, :] = jnp.zeros((1, 128), F32)
                bb[s, xs] = tmp[2 * s + xs].astype(BF16)

    def top_message(cells, a, bb, r):
        def message(step):
            dx, dy, dz = step
            if dy == 0:
                sx = {0: slice(1, 9), 1: slice(8, 9), -1: slice(1, 2)}[dx]
                tx = {0: slice(1, 9), 1: slice(0, 1), -1: slice(9, 10)}[dx]
                sz = {0: slice(128, 1152), 1: tile(8), -1: tile(1)}[dz]
                tz = {0: slice(128, 1152), 1: tile(0), -1: tile(9)}[dz]
                return cells.at[sx, :, sz], cells.at[tx, :, tz]
            s = side(dy)
            if dx == 0 and dz == 0:
                return a.at[s], r.at[s, 0:4]
            if dz == 0:
                return bb.at[s, side(dx)], r.at[s, 6 + side(dx)]
            tp = 3 if dz == 1 else 0
            slot = 4 + side(dz) if dx == 0 else 8 + 2 * side(dx) + side(dz)
            return a.at[s, tp], r.at[s, slot]

        return message

    def shift_top(cells, r, below, above):
        for x in range(10):
            for t in range(10) if x in (0, 9) else (0, 9):
                wide[t, 32 * x + 8 : 32 * x + 24, :] = cells[x, :, tile(t)].astype(F32)
        for s, row in ((0, 7), (1, 24)):
            rows = pl.ds(32 + row, 8, stride=32)
            for tp in range(4):
                both = r[s, tp].astype(F32)
                wide[2 * tp + 1, rows, :] = both[0:8]
                wide[2 * tp + 2, rows, :] = both[8:16]
            for zs, t, half in ((0, 0, 8), (1, 9, 0)):
                wide[t, rows, :] = r[s, 4 + zs].astype(F32)[half : half + 8]
            for xs, x, keep in ((0, 0, 7), (1, 9, 0)):
                at = slice(32 * x + row, 32 * x + row + 1)
                tmp[xs] = r[s, 6 + xs].astype(F32)
                for t in range(8):
                    wide[t + 1, at, :] = tmp[xs, t : t + 1, :]
                for zs, t, half in ((0, 0, 8), (1, 9, 0)):
                    tmp[2 + zs] = r[s, 8 + 2 * xs + zs].astype(F32)
                    wide[t, at, :] = tmp[2 + zs, half + keep : half + keep + 1, :]
        for x in range(10):
            for t in range(10):
                below[x, :, tile(t)] = wide[t, 32 * x + 7 : 32 * x + 23, :].astype(BF16)
                above[x, :, tile(t)] = wide[t, 32 * x + 9 : 32 * x + 25, :].astype(BF16)

    def conv_top(shifted, kernels, emit):
        @pl.loop(0, 4)
        def _(g):
            lanes = pl.ds(pl.multiple_of(256 * g, 256), 512)
            total = None
            for dx in range(3):
                for dy in range(3):
                    piece = shifted[dy][dx : dx + 8, :, lanes].reshape(128, 512)
                    term = dot(piece, kernels[3 * dx + dy])
                    total = term if total is None else total + term
            emit(g, total)

    low_half = lax.broadcasted_iota(jnp.int32, (64, 128), 1) < 64

    def band(raw, stride, first, target):
        for k in range(9):
            doubled = []
            for dz in range(3):
                at = (3 * k + dz) * stride + first
                half = raw[at : at + 64, :].astype(F32)
                doubled.append(jnp.concatenate([half, half], axis=1))
            nothing = jnp.zeros((64, 128), F32)
            pick = lambda dz: doubled[dz] if 0 <= dz < 3 else nothing
            for zi in range(8):
                for h in range(2):
                    block = jnp.where(low_half, pick(zi - 1 - 2 * h), pick(zi - 2 - 2 * h))
                    target[k, 64 * zi : 64 * zi + 64, tile(h)] = block.astype(BF16)

    vol_load.wait()
    stage_top(vol1, b["vol_a"], b["vol_b"])
    vol_x = Exchange(
        DIRS, top_message(vol1, b["vol_a"], b["vol_b"], b["vol_r"]), vol_ss, vol_rs, here, sizes
    )
    pl.semaphore_wait(barrier, greeted)
    vol_x.start()
    loads["k_top"].wait()
    band(b["k_top"], 64, 0, b["t_top"])
    loads["k_da"].wait()
    for k in range(9):
        for zi in range(4):
            for zo in range(2):
                dz = zi - zo
                if 0 <= dz < 3:
                    block = b["k_da"][64 * (3 * k + dz) : 64 * (3 * k + dz) + 64, :]
                else:
                    block = jnp.zeros((64, 128), BF16)
                b["t_da"][k, 64 * zi : 64 * zi + 64, tile(zo)] = block
    vol_x.wait_recv()
    shift_top(vol1, b["vol_r"], b["vol0"], b["vol2"])
    top_out = b["top_out"]
    skip1 = b["skip1"]

    def emit_top(g, total):
        kept = jnp.maximum(total, 0.0)
        for h in range(2):
            top_out[2 * g + h] = kept[:, tile(h)]
        skip1[1:9, :, pl.ds(pl.multiple_of(256 * g + 128, 128), 256)] = kept.astype(BF16).reshape(8, 16, 256)

    conv_top((b["vol0"], vol1, b["vol2"]), b["t_top"], emit_top)

    pm, pm_wide = b["pm"], b["pm_wide"]
    first_lanes = lax.broadcasted_iota(jnp.int32, (8, 128), 1) < 64
    for xp in range(2):
        for q in range(4):
            held = []
            for xm in (2 * xp, 2 * xp + 1):
                found = []
                for j in (2 * q, 2 * q + 1):
                    parts = [
                        top_out[j, pl.ds(16 * x + p, 8, stride=2), :]
                        for x in (2 * xm, 2 * xm + 1)
                        for p in range(2)
                    ]
                    most = jnp.maximum(jnp.maximum(parts[0], parts[1]), jnp.maximum(parts[2], parts[3]))
                    found.append(jnp.maximum(most, pltpu.roll(most, 64, 1)))
                cell = jnp.where(first_lanes, found[0], found[1])
                pm_wide[xm + 2, 2:10, tile(q + 1)] = cell
                held.append(cell)
            pm[xp + 1, q + 1] = jnp.concatenate(held, axis=0).astype(BF16)
    for s, y in ((0, 6), (1, 0)):
        for xm in range(4):
            for q in range(4):
                row = 4 * q + 2 * (xm % 2)
                b["pm_t"][s, xm // 2, row : row + 2, :] = pm_wide[xm + 2, y + 2 : y + 4, tile(q + 1)]
        for xp in range(2):
            b["pm_y"][s, xp] = b["pm_t"][s, xp].astype(BF16)

    def pm_message(step):
        dx, dy, dz = step
        if dy == 0:
            sx = {0: slice(1, 3), 1: slice(2, 3), -1: slice(1, 2)}[dx]
            tx = {0: slice(1, 3), 1: slice(0, 1), -1: slice(3, 4)}[dx]
            sz = {0: slice(1, 5), 1: slice(4, 5), -1: slice(1, 2)}[dz]
            tz = {0: slice(1, 5), 1: slice(0, 1), -1: slice(5, 6)}[dz]
            return pm.at[sx, sz], pm.at[tx, tz]
        s = side(dy)
        xs = {0: slice(0, 2), 1: slice(1, 2), -1: slice(0, 1)}[dx]
        return b["pm_y"].at[s, xs], b["pm_r"].at[s, dx + 1, dz + 1, xs]

    pm_x = Exchange(DIRS, pm_message, pm_ss, pm_rs, here, sizes)
    pm_x.start()

    stage_top(skip1, b["skip_a"], b["skip_b"])
    skip_x = Exchange(
        DIRS, top_message(skip1, b["skip_a"], b["skip_b"], b["skip_r"]), skip_ss, skip_rs, here, sizes
    )
    skip_x.start()
    loads["k_out"].wait()
    band(b["k_out"], 128, 64, b["t_skip"])

    pm_x.wait_recv()
    for xp in range(4):
        for zp in range(6):
            if 1 <= xp < 3 and 1 <= zp < 5:
                continue
            both = pm[xp, zp].astype(F32)
            pm_wide[2 * xp, 2:10, tile(zp)] = both[0:8]
            pm_wide[2 * xp + 1, 2:10, tile(zp)] = both[8:16]
    for s, y in ((0, 0), (1, 10)):
        for dx in (-1, 0, 1):
            for xp in {0: (0, 1), 1: (1,), -1: (0,)}[dx]:
                base = {0: 2 + 2 * xp, 1: 0, -1: 6}[dx]
                for dz in (-1, 0, 1):
                    slot = b["pm_t"].at[0, (dz + 1) % 2]
                    slot[...] = b["pm_r"][s, dx + 1, dz + 1, xp].astype(F32)
                    for q in {0: (0, 1, 2, 3), 1: (3,), -1: (0,)}[dz]:
                        to = {0: q + 1, 1: 0, -1: 5}[dz]
                        for xi in range(2):
                            row = 4 * q + 2 * xi
                            pm_wide[base + xi, y : y + 2, tile(to)] = slot[row : row + 2, :]
    pm_s = b["pm_s"]
    for x in range(8):
        for dy in range(3):
            pm_s[dy, x] = pm_wide[x, dy : dy + 16, :].astype(BF16)

    def flag(ok):
        return jnp.where(ok, 1.0, 0.0).astype(F32)

    def valid(at, local, size, first, index):
        place = at * local + first + index
        return flag(jnp.logical_and(place >= 0, place < local * size))

    def row_mask(rows, lanes, used, at, local, size, first):
        place = lax.broadcasted_iota(jnp.int32, (rows, lanes), 0)
        whole = place + (at * local + first)
        ok = jnp.logical_and(whole >= 0, whole < local * size)
        return jnp.logical_and(ok, place < used)

    fm_wide = b["fm_wide"]
    mid_rows = row_mask(16, 128, 10, gy, 8, sizes[1], -1)
    for j in range(5):
        total = None
        for dx in range(3):
            for dy in range(3):
                piece = pm_s[dy, dx : dx + 6, :, 128 * j : 128 * j + 256].reshape(96, 256)
                term = dot(piece, b["t_da"][3 * dx + dy])
                total = term if total is None else total + term
        total = jnp.maximum(total, 0.0)
        for x in range(6):
            for h in range(2):
                z = 2 * j + h
                keep = valid(gx, 4, sizes[0], -1, x) * valid(gz, 8, sizes[2], -1, z)
                cell = total[16 * x : 16 * x + 16, tile(h)]
                fm_wide[x, z, 0:16, :] = jnp.where(mid_rows, cell, 0.0) * keep

    def gather(wide_ref, target, xs, pairs, lanes):
        for x in range(xs):
            for zp in range(pairs):
                for dy in range(3):
                    for dz in range(3):
                        both = jnp.concatenate(
                            [wide_ref[x, 2 * zp + h + dz, dy : dy + 8, :] for h in range(2)], axis=0
                        )
                        at = (3 * dy + dz) * lanes
                        target[x, 16 * zp : 16 * zp + 16, at : at + lanes] = both.astype(BF16)

    def conv_rows(source, xs, kernels):
        rows, depth = source.shape[1], source.shape[2]
        total = None
        for dx in range(3):
            piece = source[dx : dx + xs].reshape(xs * rows, depth)
            term = dot(piece, kernels[dx * depth : (dx + 1) * depth, :])
            total = term if total is None else total + term
        return jnp.maximum(total, 0.0)

    gather(fm_wide, b["fm_s"], 6, 4, 128)
    loads["k_db"].wait()
    sm_out, sm = b["sm_out"], b["sm"]
    skip_mid = conv_rows(b["fm_s"], 4, b["k_db"])
    sm_out[...] = skip_mid.reshape(4, 8, 8, 128)
    sm[2:6, 1:5] = skip_mid.astype(BF16).reshape(4, 4, 16, 128)

    pl_t, pl_f, pl_r = b["pl_t"], b["pl_f"], b["pl_r"]
    for x in range(2):
        for z in range(4):
            parts = [sm_out[2 * x + i, 2 * z + k] for i in range(2) for k in range(2)]
            pl_t[x, z] = jnp.maximum(jnp.maximum(parts[0], parts[1]), jnp.maximum(parts[2], parts[3]))
            pl_f[x, 4 * z : 4 * z + 4, :] = jnp.maximum(
                pl_t[x, z, pl.ds(0, 4, stride=2), :], pl_t[x, z, pl.ds(1, 4, stride=2), :]
            )
        pl_r[2, 1, 1, x] = pl_f[x].astype(BF16)

    def pl_message(step):
        dx, dy, dz = step
        planes = {2: slice(1, 2), -2: slice(0, 1)}.get(dx, slice(0, 2))
        return pl_r.at[2, 1, 1, planes], pl_r.at[2 - dx, 1 - dz, 1 - dy, planes]

    pl_x = Exchange(LOW_DIRS, pl_message, pl_ss, pl_rs, here, sizes)
    pl_x.start()

    sm_t = b["sm_t"]
    for s, y in ((0, 6), (1, 0)):
        for x in range(4):
            for z in range(8):
                sm_t[x, 2 * z : 2 * z + 2, :] = sm_out[x, z, y : y + 2, :]
            b["sm_y"][s, x] = sm_t[x].astype(BF16)

    def sm_message(step):
        dx, dy, dz = step
        if dy == 0:
            sx = {0: slice(2, 6), 1: slice(4, 6), -1: slice(2, 4)}[dx]
            tx = {0: slice(2, 6), 1: slice(0, 2), -1: slice(6, 8)}[dx]
            sz = {0: slice(1, 5), 1: slice(4, 5), -1: slice(1, 2)}[dz]
            tz = {0: slice(1, 5), 1: slice(0, 1), -1: slice(5, 6)}[dz]
            return sm.at[sx, sz], sm.at[tx, tz]
        s = side(dy)
        xs = {0: slice(0, 4), 1: slice(2, 4), -1: slice(0, 2)}[dx]
        return b["sm_y"].at[s, xs], b["sm_r"].at[s, dx + 1, dz + 1, xs]

    sm_x = Exchange(DIRS, sm_message, sm_ss, sm_rs, here, sizes)
    sm_x.start()

    skip_x.wait_recv()
    shift_top(skip1, b["skip_r"], b["skip0"], b["skip2"])

    def emit_part(g, total):
        b["part"][g] = total

    conv_top((b["skip0"], skip1, b["skip2"]), b["t_skip"], emit_part)
    band(b["k_out"], 128, 0, b["t_lift"])

    pl_x.wait_recv()
    pl_wide, pl_g = b["pl_wide"], b["pl_g"]
    planes = [(0, 1), (1, 0), (1, 1), (2, 0), (2, 1), (3, 0), (3, 1), (4, 0)]
    for x, (d, p) in enumerate(planes):
        for zs in range(3):
            for ys in range(3):
                pl_g[ys] = pl_r[d, zs, ys, p].astype(F32)
            for z, to in {0: ((1, 0), (2, 1), (3, 2)), 1: ((0, 3), (1, 4), (2, 5), (3, 6)), 2: ((0, 7), (1, 8), (2, 9))}[zs]:
                pl_wide[x, to, 0:3, :] = pl_g[0, 4 * z + 1 : 4 * z + 4, :]
                pl_wide[x, to, 3:7, :] = pl_g[1, 4 * z : 4 * z + 4, :]
                pl_wide[x, to, 7:10, :] = pl_g[2, 4 * z : 4 * z + 3, :]
    gather(pl_wide, b["pl_s"], 8, 4, 128)
    loads["k_la"].wait()
    first_low = conv_rows(b["pl_s"], 6, b["k_la"])
    fl_wide = b["fl_wide"]
    low_rows = row_mask(8, 256, 8, gy, 4, sizes[1], -2)
    for x in range(6):
        for z in range(8):
            keep = valid(gx, 2, sizes[0], -2, x) * valid(gz, 4, sizes[2], -2, z)
            at = 64 * x + 8 * z
            fl_wide[x, z, 0:8, :] = jnp.where(low_rows, first_low[at : at + 8, :], 0.0) * keep
            fl_wide[x, z, 8:16, :] = jnp.zeros((8, 256), F32)
    gather(fl_wide, b["fl_s"], 6, 3, 256)
    loads["k_lb"].wait()
    coarse = conv_rows(b["fl_s"], 4, b["k_lb"])
    coarse_rows = row_mask(8, 256, 6, gy, 4, sizes[1], -1)
    cells = []
    for x in range(4):
        for z in range(6):
            keep = valid(gx, 2, sizes[0], -1, x) * valid(gz, 4, sizes[2], -1, z)
            at = 48 * x + 8 * z
            cells.append(jnp.where(coarse_rows, coarse[at : at + 8, :], 0.0) * keep)
    coarse = jnp.concatenate(cells, axis=0).astype(BF16)

    jm_wide, jm_s = b["jm_wide"], b["jm_s"]
    loads["k_ll"].wait()
    lifted = dot(coarse, b["k_ll"][...])
    for x in range(4):
        for z in range(6):
            for i in range(2):
                for h in range(2):
                    for k in range(2):
                        at = 48 * x + 8 * z
                        jm_wide[0, 2 * x + i, 2 * z + k, pl.ds(h, 8, stride=2), :] = lifted[
                            at : at + 8, tile(4 * i + 2 * h + k)
                        ]

    sm_x.wait_recv()
    for x in range(8):
        for zp in range(6):
            both = sm[x, zp].astype(F32)
            for h in range(2):
                jm_wide[1, x, 2 * zp + h, 2:10, :] = both[8 * h : 8 * h + 8]
    for s, y in ((0, 0), (1, 10)):
        for dx in (-1, 0, 1):
            for xi in {0: (0, 1, 2, 3), 1: (2, 3), -1: (0, 1)}[dx]:
                x = {0: 2 + xi, 1: xi - 2, -1: 6 + xi}[dx]
                for dz in (-1, 0, 1):
                    slot = sm_t.at[dz + 1]
                    slot[...] = b["sm_r"][s, dx + 1, dz + 1, xi].astype(F32)
                    for z in {0: range(8), 1: (6, 7), -1: (0, 1)}[dz]:
                        to = {0: z + 2, 1: z - 6, -1: 10 + z}[dz]
                        jm_wide[1, x, to, y : y + 2, :] = slot[2 * z : 2 * z + 2, :]
    for x in range(8):
        for z in range(12):
            for dy in range(3):
                for h in range(2):
                    jm_s[dy, x, z, :, tile(h)] = jm_wide[h, x, z, dy : dy + 16, :].astype(BF16)

    mg_wide = b["mg_wide"]
    mg_wide[...] = jnp.zeros(mg_wide.shape, F32)
    loads["k_um"].wait()

    @pl.loop(0, 6)
    def _(x):
        total = None
        for dx in range(3):
            for dy in range(3):
                for dz in range(3):
                    piece = jm_s[dy, x + dx, dz : dz + 10].reshape(160, 256)
                    at = 256 * (9 * dx + 3 * dy + dz)
                    term = dot(piece, b["k_um"][at : at + 256, :])
                    total = term if total is None else total + term
        total = jnp.maximum(total, 0.0)
        inside = valid(gx, 4, sizes[0], -1, x)
        for z in range(10):
            keep = inside * valid(gz, 8, sizes[2], -1, z)
            cell = jnp.where(mid_rows, total[16 * z : 16 * z + 16, :], 0.0) * keep
            for h in range(2):
                mg_wide[h, x, z, pl.ds(h, 16, stride=2), :] = cell

    t_lt = b["t_lt"]
    loads["k_lt"].wait()
    for i in range(2):
        for h in range(2):
            t_lt[128 * h : 128 * h + 128, tile(i)] = b["k_lt"][:, tile(2 * i + h)]
    lift = (b["lift0"], b["lift1"], b["lift2"])
    for x in range(6):
        for dy in range(3):
            halves = [mg_wide[h, x, :, dy + 1 : dy + 17, :].astype(BF16).reshape(160, 128) for h in range(2)]
            piece = jnp.concatenate(halves, axis=1)
            value = dot(piece, t_lt[...]).astype(BF16)
            for i in range(2):
                to = 2 * x + i - 1
                if 0 <= to < 10:
                    for z in range(10):
                        lift[dy][to, :, tile(z)] = value[16 * z : 16 * z + 16, tile(i)]

    def emit_out(g, total):
        total = total + b["part"][g]
        out[:, :, pl.ds(pl.multiple_of(256 * g, 256), 256)] = total.astype(BF16).reshape(8, 16, 256)

    conv_top(lift, b["t_lift"], emit_out)
    for exchange in (vol_x, pm_x, skip_x, pl_x, sm_x):
        exchange.wait_send()


def body(sizes, volume, *weights):
    shapes = ((1728, 64), (1728, 128), (3456, 128), (3456, 256), (6912, 256), (256, 1024), (6912, 128), (128, 512), (3456, 64))
    flat = [w.reshape(s) for w, s in zip(weights, shapes)]
    any_space = pl.BlockSpec(memory_space=pl.ANY)
    few, many = len(DIRS), len(LOW_DIRS)
    counts = (10, few, few, few, few, few, few, few, few, many, many)
    return pl.pallas_call(
        functools.partial(kernel, sizes),
        out_shape=jax.ShapeDtypeStruct(volume.shape, BF16),
        in_specs=[any_space] * 10,
        out_specs=pl.BlockSpec(memory_space=pltpu.VMEM),
        scratch_shapes=[pltpu.VMEM(s, d) for s, d in SCRATCH.values()]
        + [pltpu.SemaphoreType.DMA((c,)) for c in counts],
        compiler_params=pltpu.CompilerParams(
            collective_id=0, has_side_effects=True, vmem_limit_bytes=56 * 1024 * 1024
        ),
    )(volume, *flat)


def solution(mesh):
    placed = (P("gx", "gy", "gz"),) + (P(),) * 9
    sizes = tuple(mesh.shape[name] for name in ("gx", "gy", "gz"))
    return jax.shard_map(
        functools.partial(body, sizes),
        mesh=mesh,
        in_specs=placed,
        out_specs=P("gx", "gy", "gz"),
        check_vma=False,
    )
```

time: 235 us -> 51.7 us (0.22)
  starting transfers between devices: 105 us -> 0 us
  waiting for transfers between devices: 66.7 us -> 0 us
  Pallas kernels: 0 us -> 43.7 us
  matrix products: 25.1 us -> 0 us
  local copies, waits for them, and re-layouts: 22.7 us -> 7.77 us
  other arithmetic: 11.4 us -> 0 us
    ppermute x42 -> x0, starting transfers between devices: 105 us -> none  [the longest x21 73.4 us: padded_2(): lax.ppermute(tail, axis, [(i, (i + 1) % count) for i in range(ends)])]
    ppermute x42 -> x0, waiting for transfers between devices: 66.7 us -> none  [the longest x21 66 us: padded_2(): lax.ppermute(head, axis, [((i + 1) % count, i) for i in range(ends)])]
    pallas_call x0 -> x1, Pallas kernels: none -> 43.7 us  [body(): pl.pallas_call(functools.partial(kernel, sizes), out_shape=jax.ShapeDtype...]
    dot_general x63 -> x0, matrix products: 25.1 us -> none  [the longest x61 24.2 us: conv_valid(): total = total + jnp.dot(piece, kernel, preferred_element_type=jnp.float32)]
    slice x36 -> x0, local copies, waits for them, and re-layouts: 11 us -> none  [the longest x16 5 us: conv_valid(): kernel = weight[shift_x, shift_y].reshape(3 * inputs, outputs)]
    concatenate x9 -> x0, other arithmetic: 9.47 us -> none  [the longest x7 9.4 us: conv_valid(): jnp.concatenate([padded[:, :, depth:depth + size_z, :] for depth in range...]
    reshape x23 -> x2, local copies, waits for them, and re-layouts: 9.85 us -> 3.85 us  [body(): flat = [w.reshape(s) for w, s in zip(weights, shapes)]]
    unnamed x28 -> x2, local copies, waits for them, and re-layouts: 0.16 us -> 3.92 us
  transfers between devices with their start and end apart: 42 -> 0, of which waited for: 22 -> 0; matrix products, arithmetic and copies ran while one was open for 3% -> 0% of each run, Pallas kernels for 0% -> 0%
where the time goes in v1:
time: 51.7 us; the launch traced here: 51.5 us
  Pallas kernels  43.7 us (85%)
  local copies, waits for them, and re-layouts  7.77 us (15%)
    pallas_call x1, Pallas kernels, body(): pl.pallas_call(functools.partial(kernel, sizes), out_shape=jax.ShapeDtype...  43.7 us
    unnamed x2, local copies, waits for them, and re-layouts  3.92 us
    reshape x2, local copies, waits for them, and re-layouts, body(): flat = [w.reshape(s) for w, s in zip(weights, shapes)]  3.85 us

profile of v1, /device:TPU:1, one launch (start us, length us, event | category | flops | bytes accessed | tf_op | source)
XLA Modules:
  0.0 51.5 jit_solution(14592342160350434744)
XLA Ops:
  0.0 1.7 %copy.14.refs_8_ = bf16[128,512]{1,0:T(8,128)(2,1)} copy(bf16[128,512]{0,1:T(8,128)(2,1)} %bitcast.15) | data formatting | bytes 262144 | tf_op jit(solution)/shard_map/reshape | solution.py:626
  1.7 2.2 %reshape.32.refs_6_ = bf16[256,1024]{1,0:T(8,128)(2,1)} reshape(bf16[256,2,2,2,128]{4,3,2,1,0:T(2,128)(2,1)} %param.16) | data formatting | bytes 1048576 | tf_op jit(solution)/shard_map/reshape | solution.py:626
  3.9 2.2 %copy.13 = bf16[3,3,3,128,64]{4,3,2,1,0:T(8,128)(2,1)} copy(bf16[3,3,3,128,64]{3,4,2,1,0:T(8,128)(2,1)} %param.19) | data formatting | bytes 884736 | tf_op args[9]
  6.1 43.7 %shard_map.100 = bf16[8,16,1024]{2,1,0:T(8,128)(2,1)} custom-call(bf16[8,16,1024]{2,1,0:T(8,128)(2,1)} %refs_0_.1, bf16[1728,64]{1,0:T(8,128)(2,1)} %bitcast.13, bf16[1728,128]{1,0:T(8,128)(2,1)} %bitcast.14, bf16[3456,128]{1,0:T(8,128)(2,1)} %bitcast.12, bf16[3456,256]{1,0:T(8,128)(2,1)} %bitcast.10, bf16[6912,256]{1,0:T(8,128)(2,1)} %bitcast.8, ...), custom_call_target="tpu_custom_call" | custom-call | tf_op jit(solution)/shard_map/pallas_call | solution.py:630
  49.8 1.7 %copy.16 = bf16[8,16,1024]{2,1,0:T(8,128)(2,1)} copy(bf16[8,16,1024]{2,1,0:T(8,128)(2,1)} %shard_map.100) | data formatting | bytes 524288

commit v2 on v1

--- a/solution.py
+++ b/solution.py
@@ -11,20 +11,20 @@
 BF16 = jnp.bfloat16
 MESH = pl.DeviceIdType.MESH
 
-DIRS = [
-    (dx, dy, dz)
-    for dx in (0, -1, 1)
-    for dz in (0, -1, 1)
-    for dy in (0, -1, 1)
-    if (dx, dy, dz) != (0, 0, 0)
-]
-LOW_DIRS = [
-    (dx, dy, dz)
-    for dx in (0, -1, 1, -2, 2)
-    for dz in (0, -1, 1)
-    for dy in (0, -1, 1)
-    if (dx, dy, dz) != (0, 0, 0)
-]
+
+def directions(far):
+    steps = [
+        (dx, dy, dz)
+        for dx in range(-far, far + 1)
+        for dy in (-1, 0, 1)
+        for dz in (-1, 0, 1)
+        if (dx, dy, dz) != (0, 0, 0)
+    ]
+    return sorted(steps, key=lambda step: -sum(abs(s) for s in step))
+
+
+DIRS = directions(1)
+LOW_DIRS = directions(2)
 
 
 def dot(a, b):
@@ -43,13 +43,15 @@
     k_lb=((6912, 256), BF16),
     k_ll=((256, 1024), BF16),
     k_um=((6912, 128), BF16),
-    k_lt=((128, 512), BF16),
-    k_out=((3456, 64), BF16),
+    k_lt=((512, 128), BF16),
+    k_out=((1728, 128), BF16),
+    raw_ll=((256, 4, 2, 128), BF16),
     t_top=((9, 512, 256), BF16),
     t_skip=((9, 512, 256), BF16),
     t_lift=((9, 512, 256), BF16),
     t_da=((9, 256, 256), BF16),
     t_lt=((256, 256), BF16),
+    t_um=((2, 9, 512, 256), BF16),
     wide=((10, 320, 128), F32),
     vol0=((10, 16, 1280), BF16),
     vol1=((10, 16, 1280), BF16),
@@ -68,7 +70,7 @@
     skip_r=((2, 12, 16, 128), BF16),
     tmp=((4, 16, 128), F32),
     top_out=((8, 128, 128), F32),
-    part=((4, 128, 256), F32),
+    part=((512, 256), F32),
     pm=((4, 6, 16, 128), BF16),
     pm_y=((2, 2, 16, 128), BF16),
     pm_r=((2, 3, 3, 2, 16, 128), BF16),
@@ -91,11 +93,13 @@
     fl_wide=((6, 8, 16, 256), F32),
     fl_s=((6, 48, 2304), BF16),
     jm_wide=((2, 8, 12, 24, 128), F32),
-    jm_s=((3, 8, 12, 16, 256), BF16),
+    jm_s=((2, 3, 8, 16, 1536), BF16),
+    jm_part=((480, 256), F32),
     mg_wide=((2, 6, 10, 32, 128), F32),
 )
 NAMES = list(SCRATCH)
-WEIGHTS = ("k_top", "k_da", "k_db", "k_la", "k_lb", "k_ll", "k_um", "k_lt", "k_out")
+WEIGHTS = ("k_top", "k_da", "k_db", "k_la", "k_lb", "raw_ll", "k_um", "k_lt", "k_out")
+ORDER = ("k_top", "k_da", "k_out", "k_um", "raw_ll", "k_lt", "k_db", "k_la", "k_lb")
 
 
 class Exchange:
@@ -153,7 +157,8 @@
     vol_load = pltpu.make_async_copy(vol, vol1.at[1:9, :, 128:1152], load_sem.at[9])
     vol_load.start()
     loads = {}
-    for i, name in enumerate(WEIGHTS):
+    for name in ORDER:
+        i = WEIGHTS.index(name)
         loads[name] = pltpu.make_async_copy(weights[i], b[name], load_sem.at[i])
         loads[name].start()
 
@@ -171,6 +176,8 @@
         zero(b[name], slice(1, 9), everything, tile(9))
     for name in ("vol_r", "skip_r", "pm_r", "sm_r", "pl_r"):
         zero(b[name])
+    mg_wide = b["mg_wide"]
+    zero(mg_wide)
     for name, width, lo, hi in (("pm", 4, 1, 3), ("sm", 8, 2, 6)):
         zero(b[name], slice(0, lo))
         zero(b[name], slice(hi, width))
@@ -263,33 +270,46 @@
                 below[x, :, tile(t)] = wide[t, 32 * x + 7 : 32 * x + 23, :].astype(BF16)
                 above[x, :, tile(t)] = wide[t, 32 * x + 9 : 32 * x + 25, :].astype(BF16)
 
-    def conv_top(shifted, kernels, emit):
-        @pl.loop(0, 4)
-        def _(g):
-            lanes = pl.ds(pl.multiple_of(256 * g, 256), 512)
-            total = None
-            for dx in range(3):
-                for dy in range(3):
-                    piece = shifted[dy][dx : dx + 8, :, lanes].reshape(128, 512)
-                    term = dot(piece, kernels[3 * dx + dy])
-                    total = term if total is None else total + term
-            emit(g, total)
+    def conv_top(shifted, kernels):
+        total = None
+        for dx in range(3):
+            for dy in range(3):
+                piece = jnp.concatenate(
+                    [
+                        shifted[dy][dx : dx + 8, :, 256 * g : 256 * g + 512].reshape(128, 512)
+                        for g in range(4)
+                    ],
+                    axis=0,
+                )
+                term = dot(piece, kernels[3 * dx + dy])
+                total = term if total is None else total + term
+        return total
 
     low_half = lax.broadcasted_iota(jnp.int32, (64, 128), 1) < 64
 
-    def band(raw, stride, first, target):
-        for k in range(9):
-            doubled = []
-            for dz in range(3):
-                at = (3 * k + dz) * stride + first
-                half = raw[at : at + 64, :].astype(F32)
-                doubled.append(jnp.concatenate([half, half], axis=1))
-            nothing = jnp.zeros((64, 128), F32)
-            pick = lambda dz: doubled[dz] if 0 <= dz < 3 else nothing
-            for zi in range(8):
-                for h in range(2):
-                    block = jnp.where(low_half, pick(zi - 1 - 2 * h), pick(zi - 2 - 2 * h))
-                    target[k, 64 * zi : 64 * zi + 64, tile(h)] = block.astype(BF16)
+    def band(block, target, k):
+        nothing = jnp.zeros((64, 128), F32)
+        blocks = [block(dz) for dz in range(3)]
+        pick = lambda dz: blocks[dz] if 0 <= dz < 3 else nothing
+        for zi in range(8):
+            for h in range(2):
+                both = jnp.where(low_half, pick(zi - 1 - 2 * h), pick(zi - 2 - 2 * h))
+                target[k, 64 * zi : 64 * zi + 64, tile(h)] = both.astype(BF16)
+
+    def pairs(block, count, depth, target):
+        for zi in range(count):
+            for zo in range(count - 2):
+                value = block(zi - zo) if 0 <= zi - zo < 3 else jnp.zeros((depth, 128), BF16)
+                target[depth * zi : depth * zi + depth, tile(zo)] = value
+
+    eye = jnp.where(
+        lax.broadcasted_iota(jnp.int32, (128, 128), 0) == lax.broadcasted_iota(jnp.int32, (128, 128), 1),
+        1.0,
+        0.0,
+    ).astype(BF16)
+
+    def turned(block):
+        return lax.dot_general(eye, block, (((1,), (1,)), ((), ())), preferred_element_type=F32)
 
     vol_load.wait()
     stage_top(vol1, b["vol_a"], b["vol_b"])
@@ -299,29 +319,32 @@
     pl.semaphore_wait(barrier, greeted)
     vol_x.start()
     loads["k_top"].wait()
-    band(b["k_top"], 64, 0, b["t_top"])
+    for k in range(9):
+
+        def top_block(dz, k=k):
+            half = b["k_top"][64 * (3 * k + dz) : 64 * (3 * k + dz) + 64, :].astype(F32)
+            return jnp.concatenate([half, half], axis=1)
+
+        band(top_block, b["t_top"], k)
     loads["k_da"].wait()
     for k in range(9):
-        for zi in range(4):
-            for zo in range(2):
-                dz = zi - zo
-                if 0 <= dz < 3:
-                    block = b["k_da"][64 * (3 * k + dz) : 64 * (3 * k + dz) + 64, :]
-                else:
-                    block = jnp.zeros((64, 128), BF16)
-                b["t_da"][k, 64 * zi : 64 * zi + 64, tile(zo)] = block
+        pairs(
+            lambda dz, k=k: b["k_da"][64 * (3 * k + dz) : 64 * (3 * k + dz) + 64, :],
+            4,
+            64,
+            b["t_da"].at[k],
+        )
     vol_x.wait_recv()
     shift_top(vol1, b["vol_r"], b["vol0"], b["vol2"])
     top_out = b["top_out"]
     skip1 = b["skip1"]
 
-    def emit_top(g, total):
-        kept = jnp.maximum(total, 0.0)
+    kept = jnp.maximum(conv_top((b["vol0"], vol1, b["vol2"]), b["t_top"]), 0.0)
+    for g in range(4):
+        block = kept[128 * g : 128 * g + 128]
         for h in range(2):
-            top_out[2 * g + h] = kept[:, tile(h)]
-        skip1[1:9, :, pl.ds(pl.multiple_of(256 * g + 128, 128), 256)] = kept.astype(BF16).reshape(8, 16, 256)
-
-    conv_top((b["vol0"], vol1, b["vol2"]), b["t_top"], emit_top)
+            top_out[2 * g + h] = block[:, tile(h)]
+        skip1[1:9, :, 256 * g + 128 : 256 * g + 384] = block.astype(BF16).reshape(8, 16, 256)
 
     pm, pm_wide = b["pm"], b["pm_wide"]
     first_lanes = lax.broadcasted_iota(jnp.int32, (8, 128), 1) < 64
@@ -371,7 +394,34 @@
     )
     skip_x.start()
     loads["k_out"].wait()
-    band(b["k_out"], 128, 64, b["t_skip"])
+    for k in range(9):
+        turns = []
+        for dz in range(3):
+            block = b["k_out"][64 * (3 * k + dz) : 64 * (3 * k + dz) + 64, :]
+            turns.append(turned(jnp.concatenate([block, block], axis=0)))
+        band(lambda dz: turns[dz][0:64], b["t_lift"], k)
+        band(lambda dz: turns[dz][64:128], b["t_skip"], k)
+    loads["k_um"].wait()
+    for half in range(2):
+        for k in range(9):
+
+            def up_block(dz, half=half, k=k):
+                at = 256 * (3 * k + dz) + 128 * half
+                return b["k_um"][at : at + 128, :]
+
+            pairs(up_block, 4, 128, b["t_um"].at[half, k])
+    loads["raw_ll"].wait()
+    for q in range(0, 256, 64):
+        raw = b["raw_ll"][q : q + 64].astype(F32)
+        for i in range(4):
+            for k in range(2):
+                b["k_ll"][q : q + 64, tile(2 * i + k)] = raw[:, i, k, :].astype(BF16)
+    t_lt = b["t_lt"]
+    loads["k_lt"].wait()
+    for i in range(2):
+        for h in range(2):
+            at = 128 * (2 * i + h)
+            t_lt[128 * h : 128 * h + 128, tile(i)] = turned(b["k_lt"][at : at + 128, :]).astype(BF16)
 
     pm_x.wait_recv()
     for xp in range(4):
@@ -413,20 +463,22 @@
 
     fm_wide = b["fm_wide"]
     mid_rows = row_mask(16, 128, 10, gy, 8, sizes[1], -1)
-    for j in range(5):
-        total = None
-        for dx in range(3):
-            for dy in range(3):
-                piece = pm_s[dy, dx : dx + 6, :, 128 * j : 128 * j + 256].reshape(96, 256)
-                term = dot(piece, b["t_da"][3 * dx + dy])
-                total = term if total is None else total + term
-        total = jnp.maximum(total, 0.0)
-        for x in range(6):
-            for h in range(2):
-                z = 2 * j + h
-                keep = valid(gx, 4, sizes[0], -1, x) * valid(gz, 8, sizes[2], -1, z)
-                cell = total[16 * x : 16 * x + 16, tile(h)]
-                fm_wide[x, z, 0:16, :] = jnp.where(mid_rows, cell, 0.0) * keep
+    first_mid = None
+    for dx in range(3):
+        for dy in range(3):
+            piece = jnp.concatenate(
+                [pm_s[dy, dx : dx + 6, :, 128 * j : 128 * j + 256].reshape(96, 256) for j in range(5)],
+                axis=0,
+            )
+            term = dot(piece, b["t_da"][3 * dx + dy])
+            first_mid = term if first_mid is None else first_mid + term
+    first_mid = jnp.maximum(first_mid, 0.0)
+    for x in range(6):
+        for z in range(10):
+            keep = valid(gx, 4, sizes[0], -1, x) * valid(gz, 8, sizes[2], -1, z)
+            at = 96 * (z // 2) + 16 * x
+            cell = first_mid[at : at + 16, tile(z % 2)]
+            fm_wide[x, z, 0:16, :] = jnp.where(mid_rows, cell, 0.0) * keep
 
     def gather(wide_ref, target, xs, pairs, lanes):
         for x in range(xs):
@@ -454,24 +506,6 @@
     skip_mid = conv_rows(b["fm_s"], 4, b["k_db"])
     sm_out[...] = skip_mid.reshape(4, 8, 8, 128)
     sm[2:6, 1:5] = skip_mid.astype(BF16).reshape(4, 4, 16, 128)
-
-    pl_t, pl_f, pl_r = b["pl_t"], b["pl_f"], b["pl_r"]
-    for x in range(2):
-        for z in range(4):
-            parts = [sm_out[2 * x + i, 2 * z + k] for i in range(2) for k in range(2)]
-            pl_t[x, z] = jnp.maximum(jnp.maximum(parts[0], parts[1]), jnp.maximum(parts[2], parts[3]))
-            pl_f[x, 4 * z : 4 * z + 4, :] = jnp.maximum(
-                pl_t[x, z, pl.ds(0, 4, stride=2), :], pl_t[x, z, pl.ds(1, 4, stride=2), :]
-            )
-        pl_r[2, 1, 1, x] = pl_f[x].astype(BF16)
-
-    def pl_message(step):
-        dx, dy, dz = step
-        planes = {2: slice(1, 2), -2: slice(0, 1)}.get(dx, slice(0, 2))
-        return pl_r.at[2, 1, 1, planes], pl_r.at[2 - dx, 1 - dz, 1 - dy, planes]
-
-    pl_x = Exchange(LOW_DIRS, pl_message, pl_ss, pl_rs, here, sizes)
-    pl_x.start()
 
     sm_t = b["sm_t"]
     for s, y in ((0, 6), (1, 0)):
@@ -495,14 +529,70 @@
     sm_x = Exchange(DIRS, sm_message, sm_ss, sm_rs, here, sizes)
     sm_x.start()
 
+    pl_t, pl_f, pl_r = b["pl_t"], b["pl_f"], b["pl_r"]
+    for x in range(2):
+        for z in range(4):
+            parts = [sm_out[2 * x + i, 2 * z + k] for i in range(2) for k in range(2)]
+            pl_t[x, z] = jnp.maximum(jnp.maximum(parts[0], parts[1]), jnp.maximum(parts[2], parts[3]))
+            pl_f[x, 4 * z : 4 * z + 4, :] = jnp.maximum(
+                pl_t[x, z, pl.ds(0, 4, stride=2), :], pl_t[x, z, pl.ds(1, 4, stride=2), :]
+            )
+        pl_r[2, 1, 1, x] = pl_f[x].astype(BF16)
+
+    def pl_message(step):
+        dx, dy, dz = step
+        planes = {2: slice(1, 2), -2: slice(0, 1)}.get(dx, slice(0, 2))
+        return pl_r.at[2, 1, 1, planes], pl_r.at[2 - dx, 1 - dz, 1 - dy, planes]
+
+    pl_x = Exchange(LOW_DIRS, pl_message, pl_ss, pl_rs, here, sizes)
+    pl_x.start()
+
     skip_x.wait_recv()
     shift_top(skip1, b["skip_r"], b["skip0"], b["skip2"])
 
-    def emit_part(g, total):
-        b["part"][g] = total
-
-    conv_top((b["skip0"], skip1, b["skip2"]), b["t_skip"], emit_part)
-    band(b["k_out"], 128, 0, b["t_lift"])
+    b["part"][...] = conv_top((b["skip0"], skip1, b["skip2"]), b["t_skip"])
+
+    jm_wide, jm_s = b["jm_wide"], b["jm_s"]
+    sm_x.wait_recv()
+    for x in range(8):
+        for zp in range(6):
+            both = sm[x, zp].astype(F32)
+            for h in range(2):
+                jm_wide[1, x, 2 * zp + h, 2:10, :] = both[8 * h : 8 * h + 8]
+    for s, y in ((0, 0), (1, 10)):
+        for dx in (-1, 0, 1):
+            for xi in {0: (0, 1, 2, 3), 1: (2, 3), -1: (0, 1)}[dx]:
+                x = {0: 2 + xi, 1: xi - 2, -1: 6 + xi}[dx]
+                for dz in (-1, 0, 1):
+                    slot = sm_t.at[dz + 1]
+                    slot[...] = b["sm_r"][s, dx + 1, dz + 1, xi].astype(F32)
+                    for z in {0: range(8), 1: (6, 7), -1: (0, 1)}[dz]:
+                        to = {0: z + 2, 1: z - 6, -1: 10 + z}[dz]
+                        jm_wide[1, x, to, y : y + 2, :] = slot[2 * z : 2 * z + 2, :]
+
+    def shift_mid(half):
+        for x in range(8):
+            for z in range(12):
+                for dy in range(3):
+                    jm_s[half, dy, x, :, tile(z)] = jm_wide[half, x, z, dy : dy + 16, :].astype(BF16)
+
+    def conv_mid(half):
+        total = None
+        for dx in range(3):
+            for dy in range(3):
+                piece = jnp.concatenate(
+                    [
+                        jm_s[half, dy, dx : dx + 6, :, 256 * j : 256 * j + 512].reshape(96, 512)
+                        for j in range(5)
+                    ],
+                    axis=0,
+                )
+                term = dot(piece, b["t_um"][half, 3 * dx + dy])
+                total = term if total is None else total + term
+        return total
+
+    shift_mid(1)
+    b["jm_part"][...] = conv_mid(1)
 
     pl_x.wait_recv()
     pl_wide, pl_g = b["pl_wide"], b["pl_g"]
@@ -538,8 +628,6 @@
             cells.append(jnp.where(coarse_rows, coarse[at : at + 8, :], 0.0) * keep)
     coarse = jnp.concatenate(cells, axis=0).astype(BF16)
 
-    jm_wide, jm_s = b["jm_wide"], b["jm_s"]
-    loads["k_ll"].wait()
     lifted = dot(coarse, b["k_ll"][...])
     for x in range(4):
         for z in range(6):
@@ -551,55 +639,17 @@
                             at : at + 8, tile(4 * i + 2 * h + k)
                         ]
 
-    sm_x.wait_recv()
-    for x in range(8):
-        for zp in range(6):
-            both = sm[x, zp].astype(F32)
-            for h in range(2):
-                jm_wide[1, x, 2 * zp + h, 2:10, :] = both[8 * h : 8 * h + 8]
-    for s, y in ((0, 0), (1, 10)):
-        for dx in (-1, 0, 1):
-            for xi in {0: (0, 1, 2, 3), 1: (2, 3), -1: (0, 1)}[dx]:
-                x = {0: 2 + xi, 1: xi - 2, -1: 6 + xi}[dx]
-                for dz in (-1, 0, 1):
-                    slot = sm_t.at[dz + 1]
-                    slot[...] = b["sm_r"][s, dx + 1, dz + 1, xi].astype(F32)
-                    for z in {0: range(8), 1: (6, 7), -1: (0, 1)}[dz]:
-                        to = {0: z + 2, 1: z - 6, -1: 10 + z}[dz]
-                        jm_wide[1, x, to, y : y + 2, :] = slot[2 * z : 2 * z + 2, :]
-    for x in range(8):
-        for z in range(12):
-            for dy in range(3):
-                for h in range(2):
-                    jm_s[dy, x, z, :, tile(h)] = jm_wide[h, x, z, dy : dy + 16, :].astype(BF16)
-
     mg_wide = b["mg_wide"]
-    mg_wide[...] = jnp.zeros(mg_wide.shape, F32)
-    loads["k_um"].wait()
-
-    @pl.loop(0, 6)
-    def _(x):
-        total = None
-        for dx in range(3):
-            for dy in range(3):
-                for dz in range(3):
-                    piece = jm_s[dy, x + dx, dz : dz + 10].reshape(160, 256)
-                    at = 256 * (9 * dx + 3 * dy + dz)
-                    term = dot(piece, b["k_um"][at : at + 256, :])
-                    total = term if total is None else total + term
-        total = jnp.maximum(total, 0.0)
-        inside = valid(gx, 4, sizes[0], -1, x)
+    shift_mid(0)
+    merged = jnp.maximum(conv_mid(0) + b["jm_part"][...], 0.0)
+    for x in range(6):
         for z in range(10):
-            keep = inside * valid(gz, 8, sizes[2], -1, z)
-            cell = jnp.where(mid_rows, total[16 * z : 16 * z + 16, :], 0.0) * keep
+            keep = valid(gx, 4, sizes[0], -1, x) * valid(gz, 8, sizes[2], -1, z)
+            at = 96 * (z // 2) + 16 * x
+            cell = jnp.where(mid_rows, merged[at : at + 16, tile(z % 2)], 0.0) * keep
             for h in range(2):
                 mg_wide[h, x, z, pl.ds(h, 16, stride=2), :] = cell
 
-    t_lt = b["t_lt"]
-    loads["k_lt"].wait()
-    for i in range(2):
-        for h in range(2):
-            t_lt[128 * h : 128 * h + 128, tile(i)] = b["k_lt"][:, tile(2 * i + h)]
     lift = (b["lift0"], b["lift1"], b["lift2"])
     for x in range(6):
         for dy in range(3):
@@ -612,18 +662,26 @@
                     for z in range(10):
                         lift[dy][to, :, tile(z)] = value[16 * z : 16 * z + 16, tile(i)]
 
-    def emit_out(g, total):
-        total = total + b["part"][g]
-        out[:, :, pl.ds(pl.multiple_of(256 * g, 256), 256)] = total.astype(BF16).reshape(8, 16, 256)
-
-    conv_top(lift, b["t_lift"], emit_out)
+    total = conv_top(lift, b["t_lift"]) + b["part"][...]
+    for g in range(4):
+        out[:, :, 256 * g : 256 * g + 256] = total[128 * g : 128 * g + 128].astype(BF16).reshape(8, 16, 256)
     for exchange in (vol_x, pm_x, skip_x, pl_x, sm_x):
         exchange.wait_send()
 
 
 def body(sizes, volume, *weights):
-    shapes = ((1728, 64), (1728, 128), (3456, 128), (3456, 256), (6912, 256), (256, 1024), (6912, 128), (128, 512), (3456, 64))
-    flat = [w.reshape(s) for w, s in zip(weights, shapes)]
+    w_top, w_da, w_db, w_la, w_lb, w_ll, w_um, w_lt, w_out = weights
+    flat = [
+        w_top.reshape(1728, 64),
+        w_da.reshape(1728, 128),
+        w_db.reshape(3456, 128),
+        w_la.reshape(3456, 256),
+        w_lb.reshape(6912, 256),
+        w_ll.reshape(256, 4, 2, 128),
+        w_um.reshape(6912, 128),
+        w_lt.transpose(1, 2, 3, 4, 0).reshape(512, 128),
+        w_out.swapaxes(3, 4).reshape(1728, 128),
+    ]
     any_space = pl.BlockSpec(memory_space=pl.ANY)
     few, many = len(DIRS), len(LOW_DIRS)
     counts = (10, few, few, few, few, few, few, few, few, many, many)

time: 51.7 us -> 44.1 us (0.85)
  local copies, waits for them, and re-layouts: 7.77 us -> 1.67 us
  Pallas kernels: 43.7 us -> 42.4 us
    reshape x2 -> x0, local copies, waits for them, and re-layouts: 3.85 us -> none  [body(): flat = [w.reshape(s) for w, s in zip(weights, shapes)]]
    unnamed x2 -> x1, local copies, waits for them, and re-layouts: 3.92 us -> 1.67 us
    pallas_call x1, Pallas kernels: 43.7 us -> 42.4 us  [body(): pl.pallas_call(functools.partial(kernel, sizes), out_shape=jax.ShapeDtype...]
where the time goes in v2:
time: 44.1 us; the launch traced here: 44 us
  Pallas kernels  42.4 us (96%)
  local copies, waits for them, and re-layouts  1.67 us (4%)
    pallas_call x1, Pallas kernels, body(): pl.pallas_call(functools.partial(kernel, sizes), out_shape=jax.ShapeDtype...  42.4 us
    unnamed x1, local copies, waits for them, and re-layouts  1.67 us

profile of v2, /device:TPU:1, one launch (start us, length us, event | category | flops | bytes accessed | tf_op | source)
XLA Modules:
  0.0 44.0 jit_solution(7768654183733908536)
XLA Ops:
  0.0 42.4 %shard_map.100 = bf16[8,16,1024]{2,1,0:T(8,128)(2,1)} custom-call(bf16[8,16,1024]{2,1,0:T(8,128)(2,1)} %refs_0_.1, bf16[1728,64]{1,0:T(8,128)(2,1)} %bitcast.18, bf16[1728,128]{1,0:T(8,128)(2,1)} %bitcast.19, bf16[3456,128]{1,0:T(8,128)(2,1)} %bitcast.16, bf16[3456,256]{1,0:T(8,128)(2,1)} %bitcast.14, bf16[6912,256]{1,0:T(8,128)(2,1)} %bitcast.13, ...), custom_call_target="tpu_custom_call" | custom-call | tf_op jit(solution)/shard_map/pallas_call | solution.py:688
  42.4 1.7 %copy.12 = bf16[8,16,1024]{2,1,0:T(8,128)(2,1)} copy(bf16[8,16,1024]{2,1,0:T(8,128)(2,1)} %shard_map.100) | data formatting | bytes 524288

commit v3 on v2

--- a/solution.py
+++ b/solution.py
@@ -99,7 +99,7 @@
 )
 NAMES = list(SCRATCH)
 WEIGHTS = ("k_top", "k_da", "k_db", "k_la", "k_lb", "raw_ll", "k_um", "k_lt", "k_out")
-ORDER = ("k_top", "k_da", "k_out", "k_um", "raw_ll", "k_lt", "k_db", "k_la", "k_lb")
+ORDER = ("k_top", "k_da", "raw_ll", "k_out", "k_um", "k_db", "k_lt", "k_la", "k_lb")
 
 
 class Exchange:
@@ -156,11 +156,6 @@
     vol1 = b["vol1"]
     vol_load = pltpu.make_async_copy(vol, vol1.at[1:9, :, 128:1152], load_sem.at[9])
     vol_load.start()
-    loads = {}
-    for name in ORDER:
-        i = WEIGHTS.index(name)
-        loads[name] = pltpu.make_async_copy(weights[i], b[name], load_sem.at[i])
-        loads[name].start()
 
     def zero(ref, *at):
         if at:
@@ -196,6 +191,12 @@
                 device_id=tuple(at + s for at, s in zip(here, step)),
                 device_id_type=MESH,
             )
+
+    loads = {}
+    for name in ORDER:
+        i = WEIGHTS.index(name)
+        loads[name] = pltpu.make_async_copy(weights[i], b[name], load_sem.at[i])
+        loads[name].start()
 
     def reach(at, size, far):
         count = jnp.int32(1)
@@ -334,6 +335,20 @@
             64,
             b["t_da"].at[k],
         )
+    loads["raw_ll"].wait()
+    for q in range(0, 256, 64):
+        raw = b["raw_ll"][q : q + 64].astype(F32)
+        for i in range(4):
+            for k in range(2):
+                b["k_ll"][q : q + 64, tile(2 * i + k)] = raw[:, i, k, :].astype(BF16)
+    loads["k_out"].wait()
+    for k in range(9):
+        turns = []
+        for dz in range(3):
+            block = b["k_out"][64 * (3 * k + dz) : 64 * (3 * k + dz) + 64, :]
+            turns.append(turned(jnp.concatenate([block, block], axis=0)))
+        band(lambda dz: turns[dz][0:64], b["t_lift"], k)
+        band(lambda dz: turns[dz][64:128], b["t_skip"], k)
     vol_x.wait_recv()
     shift_top(vol1, b["vol_r"], b["vol0"], b["vol2"])
     top_out = b["top_out"]
@@ -393,14 +408,6 @@
         DIRS, top_message(skip1, b["skip_a"], b["skip_b"], b["skip_r"]), skip_ss, skip_rs, here, sizes
     )
     skip_x.start()
-    loads["k_out"].wait()
-    for k in range(9):
-        turns = []
-        for dz in range(3):
-            block = b["k_out"][64 * (3 * k + dz) : 64 * (3 * k + dz) + 64, :]
-            turns.append(turned(jnp.concatenate([block, block], axis=0)))
-        band(lambda dz: turns[dz][0:64], b["t_lift"], k)
-        band(lambda dz: turns[dz][64:128], b["t_skip"], k)
     loads["k_um"].wait()
     for half in range(2):
         for k in range(9):
@@ -410,19 +417,6 @@
                 return b["k_um"][at : at + 128, :]
 
             pairs(up_block, 4, 128, b["t_um"].at[half, k])
-    loads["raw_ll"].wait()
-    for q in range(0, 256, 64):
-        raw = b["raw_ll"][q : q + 64].astype(F32)
-        for i in range(4):
-            for k in range(2):
-                b["k_ll"][q : q + 64, tile(2 * i + k)] = raw[:, i, k, :].astype(BF16)
-    t_lt = b["t_lt"]
-    loads["k_lt"].wait()
-    for i in range(2):
-        for h in range(2):
-            at = 128 * (2 * i + h)
-            t_lt[128 * h : 128 * h + 128, tile(i)] = turned(b["k_lt"][at : at + 128, :]).astype(BF16)
-
     pm_x.wait_recv()
     for xp in range(4):
         for zp in range(6):
@@ -551,6 +545,13 @@
     shift_top(skip1, b["skip_r"], b["skip0"], b["skip2"])
 
     b["part"][...] = conv_top((b["skip0"], skip1, b["skip2"]), b["t_skip"])
+
+    t_lt = b["t_lt"]
+    loads["k_lt"].wait()
+    for i in range(2):
+        for h in range(2):
+            at = 128 * (2 * i + h)
+            t_lt[128 * h : 128 * h + 128, tile(i)] = turned(b["k_lt"][at : at + 128, :]).astype(BF16)
 
     jm_wide, jm_s = b["jm_wide"], b["jm_s"]
     sm_x.wait_recv()
@@ -687,7 +688,7 @@
     counts = (10, few, few, few, few, few, few, few, few, many, many)
     return pl.pallas_call(
         functools.partial(kernel, sizes),
-        out_shape=jax.ShapeDtypeStruct(volume.shape, BF16),
+        out_shape=pltpu.VMEM(volume.shape, BF16),
         in_specs=[any_space] * 10,
         out_specs=pl.BlockSpec(memory_space=pltpu.VMEM),
         scratch_shapes=[pltpu.VMEM(s, d) for s, d in SCRATCH.values()]

time: 44.1 us -> 42.8 us (0.971)
  local copies, waits for them, and re-layouts: 1.67 us -> 0.71 us
    unnamed x1, local copies, waits for them, and re-layouts: 1.67 us -> 0.71 us
where the time goes in v3:
time: 42.8 us; the launch traced here: 42.7 us
  Pallas kernels  42 us (98%)
  local copies, waits for them, and re-layouts  0.71 us (2%)
    pallas_call x1, Pallas kernels, body(): pl.pallas_call(functools.partial(kernel, sizes), out_shape=pltpu.VMEM(vol...  42 us

profile of v3, /device:TPU:1, one launch (start us, length us, event | category | flops | bytes accessed | tf_op | source)
XLA Modules:
  0.0 42.7 jit_solution(14966662795483438235)
XLA Ops:
  0.0 42.0 %shard_map.100 = bf16[8,16,1024]{2,1,0:T(8,128)(2,1)S(1)} custom-call(bf16[8,16,1024]{2,1,0:T(8,128)(2,1)} %refs_0_.1, bf16[1728,64]{1,0:T(8,128)(2,1)} %bitcast.18, bf16[1728,128]{1,0:T(8,128)(2,1)} %bitcast.19, bf16[3456,128]{1,0:T(8,128)(2,1)} %bitcast.16, bf16[3456,256]{1,0:T(8,128)(2,1)} %bitcast.14, bf16[6912,256]{1,0:T(8,128)(2,1)} %bitcast.13, ...), custom_call_target="tpu_custom_call" | custom-call | tf_op jit(solution)/shard_map/pallas_call | solution.py:689
  42.0 0.7 %copy.12 = bf16[8,16,1024]{2,1,0:T(8,128)(2,1)} copy(bf16[8,16,1024]{2,1,0:T(8,128)(2,1)S(1)} %shard_map.100) | data formatting | bytes 524288

commit v4 on v3

--- a/solution.py
+++ b/solution.py
@@ -12,19 +12,22 @@
 MESH = pl.DeviceIdType.MESH
 
 
-def directions(far):
-    steps = [
+def farthest_first(steps):
+    return sorted(steps, key=lambda step: -sum(abs(s) for s in step))
+
+
+DIRS = farthest_first(
+    [
         (dx, dy, dz)
-        for dx in range(-far, far + 1)
+        for dx in (-1, 0, 1)
         for dy in (-1, 0, 1)
         for dz in (-1, 0, 1)
         if (dx, dy, dz) != (0, 0, 0)
     ]
-    return sorted(steps, key=lambda step: -sum(abs(s) for s in step))
-
-
-DIRS = directions(1)
-LOW_DIRS = directions(2)
+)
+LINE_DIRS = farthest_first([(dx, 0, 0) for dx in (-2, -1, 1, 2)])
+PLANE_DIRS = [step for step in DIRS if step[0] == 0]
+GREETED = DIRS + LINE_DIRS[:2]
 
 
 def dot(a, b):
@@ -48,7 +51,7 @@
     raw_ll=((256, 4, 2, 128), BF16),
     t_top=((9, 512, 256), BF16),
     t_skip=((9, 512, 256), BF16),
-    t_lift=((9, 512, 256), BF16),
+    t_lift=((9, 384, 256), BF16),
     t_da=((9, 256, 256), BF16),
     t_lt=((256, 256), BF16),
     t_um=((2, 9, 512, 256), BF16),
@@ -59,9 +62,9 @@
     skip0=((10, 16, 1280), BF16),
     skip1=((10, 16, 1280), BF16),
     skip2=((10, 16, 1280), BF16),
-    lift0=((10, 16, 1280), BF16),
-    lift1=((10, 16, 1280), BF16),
-    lift2=((10, 16, 1280), BF16),
+    lift0=((10, 16, 1152), BF16),
+    lift1=((10, 16, 1152), BF16),
+    lift2=((10, 16, 1152), BF16),
     vol_a=((2, 4, 16, 128), BF16),
     vol_b=((2, 2, 16, 128), BF16),
     vol_r=((2, 12, 16, 128), BF16),
@@ -82,11 +85,14 @@
     sm_out=((4, 8, 8, 128), F32),
     sm=((8, 6, 16, 128), BF16),
     sm_y=((2, 4, 16, 128), BF16),
-    sm_r=((2, 3, 3, 4, 16, 128), BF16),
+    sm_e=((2, 2, 16, 128), BF16),
+    sm_r=((2, 3, 4, 16, 128), BF16),
+    sm_c=((2, 3, 2, 16, 128), BF16),
+    sm_u=((2, 16, 128), F32),
     sm_t=((4, 16, 128), F32),
     pl_t=((2, 4, 8, 128), F32),
     pl_f=((2, 16, 128), F32),
-    pl_r=((5, 3, 3, 2, 16, 128), BF16),
+    pl_r=((3, 3, 8, 16, 128), BF16),
     pl_g=((3, 16, 128), F32),
     pl_wide=((8, 10, 16, 128), F32),
     pl_s=((8, 64, 1152), BF16),
@@ -148,14 +154,17 @@
     vol, weights, out = refs[0], refs[1:10], refs[10]
     n = len(NAMES)
     b = dict(zip(NAMES, refs[11 : 11 + n]))
-    (load_sem, vol_ss, vol_rs, skip_ss, skip_rs, pm_ss, pm_rs, sm_ss, sm_rs, pl_ss, pl_rs) = refs[11 + n :]
+    (load_sem, vol_ss, vol_rs, skip_ss, skip_rs, pm_ss, pm_rs, sm_ss, sm_rs, line_ss, line_rs, pl_ss, pl_rs) = refs[11 + n :]
     here = tuple(lax.axis_index(name) for name in ("gx", "gy", "gz"))
     gx, gy, gz = here
     tile = lambda t: slice(128 * t, 128 * t + 128)
 
     vol1 = b["vol1"]
-    vol_load = pltpu.make_async_copy(vol, vol1.at[1:9, :, 128:1152], load_sem.at[9])
-    vol_load.start()
+    vol_loads = [
+        pltpu.make_async_copy(vol.at[x], vol1.at[x + 1, :, 128:1152], load_sem.at[9 + x]) for x in range(8)
+    ]
+    for load in vol_loads:
+        load.start()
 
     def zero(ref, *at):
         if at:
@@ -169,10 +178,8 @@
         zero(b[name], slice(9, 10))
         zero(b[name], slice(1, 9), everything, tile(0))
         zero(b[name], slice(1, 9), everything, tile(9))
-    for name in ("vol_r", "skip_r", "pm_r", "sm_r", "pl_r"):
+    for name in ("vol_r", "skip_r", "pm_r", "sm_r", "sm_c", "pl_r"):
         zero(b[name])
-    mg_wide = b["mg_wide"]
-    zero(mg_wide)
     for name, width, lo, hi in (("pm", 4, 1, 3), ("sm", 8, 2, 6)):
         zero(b[name], slice(0, lo))
         zero(b[name], slice(hi, width))
@@ -180,10 +187,10 @@
         zero(b[name], slice(lo, hi), slice(5, 6))
 
     barrier = pltpu.get_barrier_semaphore()
-    low_x = Exchange(LOW_DIRS, None, None, None, here, sizes)
-    for step in LOW_DIRS:
-
-        @pl.when(low_x.inside(step, 1))
+    greeting = Exchange(GREETED, None, None, None, here, sizes)
+    for step in GREETED:
+
+        @pl.when(greeting.inside(step, 1))
         def _(step=step):
             pl.semaphore_signal(
                 barrier,
@@ -199,12 +206,13 @@
         loads[name].start()
 
     def reach(at, size, far):
-        count = jnp.int32(1)
-        for s in range(1, far + 1):
-            count = count + jnp.where(at >= s, 1, 0) + jnp.where(at + s < size, 1, 0)
-        return count
-
-    greeted = reach(gx, sizes[0], 2) * reach(gy, sizes[1], 1) * reach(gz, sizes[2], 1) - 1
+        return jnp.where(at >= far, 1, 0) + jnp.where(at + far < size, 1, 0)
+
+    greeted = reach(gx, sizes[0], 2) - 1
+    around = 1
+    for at, size in zip(here, sizes):
+        around = around * (1 + reach(at, size, 1))
+    greeted = greeted + around
 
     wide = b["wide"]
     tmp = b["tmp"]
@@ -271,13 +279,13 @@
                 below[x, :, tile(t)] = wide[t, 32 * x + 7 : 32 * x + 23, :].astype(BF16)
                 above[x, :, tile(t)] = wide[t, 32 * x + 9 : 32 * x + 25, :].astype(BF16)
 
-    def conv_top(shifted, kernels):
+    def conv_top(shifted, kernels, depth=512):
         total = None
         for dx in range(3):
             for dy in range(3):
                 piece = jnp.concatenate(
                     [
-                        shifted[dy][dx : dx + 8, :, 256 * g : 256 * g + 512].reshape(128, 512)
+                        shifted[dy][dx : dx + 8, :, 256 * g : 256 * g + depth].reshape(128, depth)
                         for g in range(4)
                     ],
                     axis=0,
@@ -288,13 +296,13 @@
 
     low_half = lax.broadcasted_iota(jnp.int32, (64, 128), 1) < 64
 
-    def band(block, target, k):
+    def band(block, target, k, lead=1):
         nothing = jnp.zeros((64, 128), F32)
         blocks = [block(dz) for dz in range(3)]
         pick = lambda dz: blocks[dz] if 0 <= dz < 3 else nothing
-        for zi in range(8):
+        for zi in range(6 + 2 * lead):
             for h in range(2):
-                both = jnp.where(low_half, pick(zi - 1 - 2 * h), pick(zi - 2 - 2 * h))
+                both = jnp.where(low_half, pick(zi - lead - 2 * h), pick(zi - lead - 1 - 2 * h))
                 target[k, 64 * zi : 64 * zi + 64, tile(h)] = both.astype(BF16)
 
     def pairs(block, count, depth, target):
@@ -312,13 +320,16 @@
     def turned(block):
         return lax.dot_general(eye, block, (((1,), (1,)), ((), ())), preferred_element_type=F32)
 
-    vol_load.wait()
+    for load in vol_loads:
+        load.wait()
     stage_top(vol1, b["vol_a"], b["vol_b"])
     vol_x = Exchange(
         DIRS, top_message(vol1, b["vol_a"], b["vol_b"], b["vol_r"]), vol_ss, vol_rs, here, sizes
     )
     pl.semaphore_wait(barrier, greeted)
     vol_x.start()
+    mg_wide = b["mg_wide"]
+    zero(mg_wide)
     loads["k_top"].wait()
     for k in range(9):
 
@@ -347,7 +358,7 @@
         for dz in range(3):
             block = b["k_out"][64 * (3 * k + dz) : 64 * (3 * k + dz) + 64, :]
             turns.append(turned(jnp.concatenate([block, block], axis=0)))
-        band(lambda dz: turns[dz][0:64], b["t_lift"], k)
+        band(lambda dz: turns[dz][0:64], b["t_lift"], k, 0)
         band(lambda dz: turns[dz][64:128], b["t_skip"], k)
     vol_x.wait_recv()
     shift_top(vol1, b["vol_r"], b["vol0"], b["vol2"])
@@ -501,12 +512,42 @@
     sm_out[...] = skip_mid.reshape(4, 8, 8, 128)
     sm[2:6, 1:5] = skip_mid.astype(BF16).reshape(4, 4, 16, 128)
 
+    pl_t, pl_f, pl_r = b["pl_t"], b["pl_f"], b["pl_r"]
+    for x in range(2):
+        for z in range(4):
+            parts = [sm_out[2 * x + i, 2 * z + k] for i in range(2) for k in range(2)]
+            pl_t[x, z] = jnp.maximum(jnp.maximum(parts[0], parts[1]), jnp.maximum(parts[2], parts[3]))
+            pl_f[x, 4 * z : 4 * z + 4, :] = jnp.maximum(
+                pl_t[x, z, pl.ds(0, 4, stride=2), :], pl_t[x, z, pl.ds(1, 4, stride=2), :]
+            )
+        pl_r[1, 1, 3 + x] = pl_f[x].astype(BF16)
+
+    def line_message(step):
+        sx, tx = {
+            1: (slice(3, 5), slice(1, 3)),
+            -1: (slice(3, 5), slice(5, 7)),
+            2: (slice(4, 5), slice(0, 1)),
+            -2: (slice(3, 4), slice(7, 8)),
+        }[step[0]]
+        return pl_r.at[1, 1, sx], pl_r.at[1, 1, tx]
+
+    def pl_message(step):
+        return pl_r.at[1, 1], pl_r.at[1 - step[2], 1 - step[1]]
+
+    line_x = Exchange(LINE_DIRS, line_message, line_ss, line_rs, here, sizes)
+    pl_x = Exchange(PLANE_DIRS, pl_message, pl_ss, pl_rs, here, sizes)
+    line_x.start()
+
     sm_t = b["sm_t"]
     for s, y in ((0, 6), (1, 0)):
         for x in range(4):
             for z in range(8):
                 sm_t[x, 2 * z : 2 * z + 2, :] = sm_out[x, z, y : y + 2, :]
             b["sm_y"][s, x] = sm_t[x].astype(BF16)
+        for zs, z in ((0, 6), (1, 0)):
+            for x in range(4):
+                b["sm_u"][zs, 4 * x : 4 * x + 4, :] = sm_t[x, 2 * z : 2 * z + 4, :]
+            b["sm_e"][s, zs] = b["sm_u"][zs].astype(BF16)
 
     def sm_message(step):
         dx, dy, dz = step
@@ -517,41 +558,28 @@
             tz = {0: slice(1, 5), 1: slice(0, 1), -1: slice(5, 6)}[dz]
             return sm.at[sx, sz], sm.at[tx, tz]
         s = side(dy)
+        if dz != 0:
+            return b["sm_e"].at[s, side(dz)], b["sm_c"].at[s, dx + 1, side(dz)]
         xs = {0: slice(0, 4), 1: slice(2, 4), -1: slice(0, 2)}[dx]
-        return b["sm_y"].at[s, xs], b["sm_r"].at[s, dx + 1, dz + 1, xs]
+        return b["sm_y"].at[s, xs], b["sm_r"].at[s, dx + 1, xs]
 
     sm_x = Exchange(DIRS, sm_message, sm_ss, sm_rs, here, sizes)
     sm_x.start()
 
-    pl_t, pl_f, pl_r = b["pl_t"], b["pl_f"], b["pl_r"]
-    for x in range(2):
-        for z in range(4):
-            parts = [sm_out[2 * x + i, 2 * z + k] for i in range(2) for k in range(2)]
-            pl_t[x, z] = jnp.maximum(jnp.maximum(parts[0], parts[1]), jnp.maximum(parts[2], parts[3]))
-            pl_f[x, 4 * z : 4 * z + 4, :] = jnp.maximum(
-                pl_t[x, z, pl.ds(0, 4, stride=2), :], pl_t[x, z, pl.ds(1, 4, stride=2), :]
-            )
-        pl_r[2, 1, 1, x] = pl_f[x].astype(BF16)
-
-    def pl_message(step):
-        dx, dy, dz = step
-        planes = {2: slice(1, 2), -2: slice(0, 1)}.get(dx, slice(0, 2))
-        return pl_r.at[2, 1, 1, planes], pl_r.at[2 - dx, 1 - dz, 1 - dy, planes]
-
-    pl_x = Exchange(LOW_DIRS, pl_message, pl_ss, pl_rs, here, sizes)
-    pl_x.start()
-
     skip_x.wait_recv()
     shift_top(skip1, b["skip_r"], b["skip0"], b["skip2"])
 
     b["part"][...] = conv_top((b["skip0"], skip1, b["skip2"]), b["t_skip"])
+    line_x.wait_recv()
+    pl_x.start()
 
     t_lt = b["t_lt"]
     loads["k_lt"].wait()
     for i in range(2):
         for h in range(2):
             at = 128 * (2 * i + h)
-            t_lt[128 * h : 128 * h + 128, tile(i)] = turned(b["k_lt"][at : at + 128, :]).astype(BF16)
+            swapped = [b["k_lt"][at + 64 : at + 128, :], b["k_lt"][at : at + 64, :]]
+            t_lt[128 * h : 128 * h + 128, tile(i)] = turned(jnp.concatenate(swapped, axis=0)).astype(BF16)
 
     jm_wide, jm_s = b["jm_wide"], b["jm_s"]
     sm_x.wait_recv()
@@ -564,12 +592,18 @@
         for dx in (-1, 0, 1):
             for xi in {0: (0, 1, 2, 3), 1: (2, 3), -1: (0, 1)}[dx]:
                 x = {0: 2 + xi, 1: xi - 2, -1: 6 + xi}[dx]
-                for dz in (-1, 0, 1):
-                    slot = sm_t.at[dz + 1]
-                    slot[...] = b["sm_r"][s, dx + 1, dz + 1, xi].astype(F32)
-                    for z in {0: range(8), 1: (6, 7), -1: (0, 1)}[dz]:
-                        to = {0: z + 2, 1: z - 6, -1: 10 + z}[dz]
-                        jm_wide[1, x, to, y : y + 2, :] = slot[2 * z : 2 * z + 2, :]
+                slot = sm_t.at[xi % 2]
+                slot[...] = b["sm_r"][s, dx + 1, xi].astype(F32)
+                for z in range(8):
+                    jm_wide[1, x, z + 2, y : y + 2, :] = slot[2 * z : 2 * z + 2, :]
+            for zs, to in ((0, 0), (1, 10)):
+                slot = sm_t.at[2 + zs]
+                slot[...] = b["sm_c"][s, dx + 1, zs].astype(F32)
+                for xi in {0: (0, 1, 2, 3), 1: (2, 3), -1: (0, 1)}[dx]:
+                    x = {0: 2 + xi, 1: xi - 2, -1: 6 + xi}[dx]
+                    for z in range(2):
+                        row = 4 * xi + 2 * z
+                        jm_wide[1, x, to + z, y : y + 2, :] = slot[row : row + 2, :]
 
     def shift_mid(half):
         for x in range(8):
@@ -597,11 +631,10 @@
 
     pl_x.wait_recv()
     pl_wide, pl_g = b["pl_wide"], b["pl_g"]
-    planes = [(0, 1), (1, 0), (1, 1), (2, 0), (2, 1), (3, 0), (3, 1), (4, 0)]
-    for x, (d, p) in enumerate(planes):
+    for x in range(8):
         for zs in range(3):
             for ys in range(3):
-                pl_g[ys] = pl_r[d, zs, ys, p].astype(F32)
+                pl_g[ys] = pl_r[zs, ys, x].astype(F32)
             for z, to in {0: ((1, 0), (2, 1), (3, 2)), 1: ((0, 3), (1, 4), (2, 5), (3, 6)), 2: ((0, 7), (1, 8), (2, 9))}[zs]:
                 pl_wide[x, to, 0:3, :] = pl_g[0, 4 * z + 1 : 4 * z + 4, :]
                 pl_wide[x, to, 3:7, :] = pl_g[1, 4 * z : 4 * z + 4, :]
@@ -651,6 +684,7 @@
             for h in range(2):
                 mg_wide[h, x, z, pl.ds(h, 16, stride=2), :] = cell
 
+    lift_half = lax.broadcasted_iota(jnp.int32, (16, 128), 1) < 64
     lift = (b["lift0"], b["lift1"], b["lift2"])
     for x in range(6):
         for dy in range(3):
@@ -660,13 +694,17 @@
             for i in range(2):
                 to = 2 * x + i - 1
                 if 0 <= to < 10:
-                    for z in range(10):
-                        lift[dy][to, :, tile(z)] = value[16 * z : 16 * z + 16, tile(i)]
-
-    total = conv_top(lift, b["t_lift"]) + b["part"][...]
+                    for t in range(9):
+                        lift[dy][to, :, tile(t)] = jnp.where(
+                            lift_half,
+                            value[16 * t : 16 * t + 16, tile(i)],
+                            value[16 * t + 16 : 16 * t + 32, tile(i)],
+                        )
+
+    total = conv_top(lift, b["t_lift"], 384) + b["part"][...]
     for g in range(4):
         out[:, :, 256 * g : 256 * g + 256] = total[128 * g : 128 * g + 128].astype(BF16).reshape(8, 16, 256)
-    for exchange in (vol_x, pm_x, skip_x, pl_x, sm_x):
+    for exchange in (vol_x, pm_x, skip_x, line_x, pl_x, sm_x):
         exchange.wait_send()
 
 
@@ -684,8 +722,8 @@
         w_out.swapaxes(3, 4).reshape(1728, 128),
     ]
     any_space = pl.BlockSpec(memory_space=pl.ANY)
-    few, many = len(DIRS), len(LOW_DIRS)
-    counts = (10, few, few, few, few, few, few, few, few, many, many)
+    few, line, plane = len(DIRS), len(LINE_DIRS), len(PLANE_DIRS)
+    counts = (17, few, few, few, few, few, few, few, few, line, line, plane, plane)
     return pl.pallas_call(
         functools.partial(kernel, sizes),
         out_shape=pltpu.VMEM(volume.shape, BF16),

time: 42.8 us -> 41.7 us (0.974)
  Pallas kernels: 42 us -> 40.9 us
    pallas_call x1, Pallas kernels: 42 us -> 40.9 us  [body(): pl.pallas_call(functools.partial(kernel, sizes), out_shape=pltpu.VMEM(vol...]
where the time goes in v4:
time: 41.7 us; the launch traced here: 41.6 us
  Pallas kernels  40.9 us (98%)
  local copies, waits for them, and re-layouts  0.71 us (2%)
    pallas_call x1, Pallas kernels, body(): pl.pallas_call(functools.partial(kernel, sizes), out_shape=pltpu.VMEM(vol...  40.9 us

profile of v4, /device:TPU:1, one launch (start us, length us, event | category | flops | bytes accessed | tf_op | source)
XLA Modules:
  0.0 41.6 jit_solution(12564891038355082453)
XLA Ops:
  0.0 40.9 %shard_map.100 = bf16[8,16,1024]{2,1,0:T(8,128)(2,1)S(1)} custom-call(bf16[8,16,1024]{2,1,0:T(8,128)(2,1)} %refs_0_.1, bf16[1728,64]{1,0:T(8,128)(2,1)} %bitcast.18, bf16[1728,128]{1,0:T(8,128)(2,1)} %bitcast.19, bf16[3456,128]{1,0:T(8,128)(2,1)} %bitcast.16, bf16[3456,256]{1,0:T(8,128)(2,1)} %bitcast.14, bf16[6912,256]{1,0:T(8,128)(2,1)} %bitcast.13, ...), custom_call_target="tpu_custom_call" | custom-call | tf_op jit(solution)/shard_map/pallas_call | solution.py:727
  40.9 0.7 %copy.12 = bf16[8,16,1024]{2,1,0:T(8,128)(2,1)} copy(bf16[8,16,1024]{2,1,0:T(8,128)(2,1)S(1)} %shard_map.100) | data formatting | bytes 524288

commit v5 on v4

--- a/solution.py
+++ b/solution.py
@@ -13,7 +13,7 @@
 
 
 def farthest_first(steps):
-    return sorted(steps, key=lambda step: -sum(abs(s) for s in step))
+    return sorted(steps, key=lambda step: -(2 * abs(step[0]) + abs(step[1]) + 3 * abs(step[2])))
 
 
 DIRS = farthest_first(
@@ -32,6 +32,14 @@
 
 def dot(a, b):
     return jnp.dot(a, b, preferred_element_type=F32)
+
+
+def in_plane(step):
+    return step[1] == 0
+
+
+def off_plane(step):
+    return step[1] != 0
 
 
 def side(step):
@@ -81,7 +89,7 @@
     pm_wide=((8, 24, 768), F32),
     pm_s=((3, 8, 16, 768), BF16),
     fm_wide=((6, 10, 24, 128), F32),
-    fm_s=((6, 64, 1152), BF16),
+    fm_s=((2, 3, 6, 80, 128), BF16),
     sm_out=((4, 8, 8, 128), F32),
     sm=((8, 6, 16, 128), BF16),
     sm_y=((2, 4, 16, 128), BF16),
@@ -95,9 +103,9 @@
     pl_r=((3, 3, 8, 16, 128), BF16),
     pl_g=((3, 16, 128), F32),
     pl_wide=((8, 10, 16, 128), F32),
-    pl_s=((8, 64, 1152), BF16),
+    pl_s=((2, 3, 8, 80, 128), BF16),
     fl_wide=((6, 8, 16, 256), F32),
-    fl_s=((6, 48, 2304), BF16),
+    fl_s=((2, 3, 6, 64, 256), BF16),
     jm_wide=((2, 8, 12, 24, 128), F32),
     jm_s=((2, 3, 8, 16, 1536), BF16),
     jm_part=((480, 256), F32),
@@ -137,8 +145,10 @@
             device_id_type=MESH,
         )
 
-    def start(self):
+    def start(self, chosen=lambda step: True):
         for i, step in enumerate(self.dirs):
+            if not chosen(step):
+                continue
             pl.when(self.inside(step, 1))(lambda i=i: self.copy(i).start())
 
     def wait_recv(self):
@@ -346,20 +356,6 @@
             64,
             b["t_da"].at[k],
         )
-    loads["raw_ll"].wait()
-    for q in range(0, 256, 64):
-        raw = b["raw_ll"][q : q + 64].astype(F32)
-        for i in range(4):
-            for k in range(2):
-                b["k_ll"][q : q + 64, tile(2 * i + k)] = raw[:, i, k, :].astype(BF16)
-    loads["k_out"].wait()
-    for k in range(9):
-        turns = []
-        for dz in range(3):
-            block = b["k_out"][64 * (3 * k + dz) : 64 * (3 * k + dz) + 64, :]
-            turns.append(turned(jnp.concatenate([block, block], axis=0)))
-        band(lambda dz: turns[dz][0:64], b["t_lift"], k, 0)
-        band(lambda dz: turns[dz][64:128], b["t_skip"], k)
     vol_x.wait_recv()
     shift_top(vol1, b["vol_r"], b["vol0"], b["vol2"])
     top_out = b["top_out"]
@@ -391,14 +387,6 @@
                 pm_wide[xm + 2, 2:10, tile(q + 1)] = cell
                 held.append(cell)
             pm[xp + 1, q + 1] = jnp.concatenate(held, axis=0).astype(BF16)
-    for s, y in ((0, 6), (1, 0)):
-        for xm in range(4):
-            for q in range(4):
-                row = 4 * q + 2 * (xm % 2)
-                b["pm_t"][s, xm // 2, row : row + 2, :] = pm_wide[xm + 2, y + 2 : y + 4, tile(q + 1)]
-        for xp in range(2):
-            b["pm_y"][s, xp] = b["pm_t"][s, xp].astype(BF16)
-
     def pm_message(step):
         dx, dy, dz = step
         if dy == 0:
@@ -412,13 +400,36 @@
         return b["pm_y"].at[s, xs], b["pm_r"].at[s, dx + 1, dz + 1, xs]
 
     pm_x = Exchange(DIRS, pm_message, pm_ss, pm_rs, here, sizes)
-    pm_x.start()
-
-    stage_top(skip1, b["skip_a"], b["skip_b"])
+    pm_x.start(in_plane)
+    for s, y in ((0, 6), (1, 0)):
+        for xm in range(4):
+            for q in range(4):
+                row = 4 * q + 2 * (xm % 2)
+                b["pm_t"][s, xm // 2, row : row + 2, :] = pm_wide[xm + 2, y + 2 : y + 4, tile(q + 1)]
+        for xp in range(2):
+            b["pm_y"][s, xp] = b["pm_t"][s, xp].astype(BF16)
+    pm_x.start(off_plane)
+
     skip_x = Exchange(
         DIRS, top_message(skip1, b["skip_a"], b["skip_b"], b["skip_r"]), skip_ss, skip_rs, here, sizes
     )
-    skip_x.start()
+    skip_x.start(in_plane)
+    stage_top(skip1, b["skip_a"], b["skip_b"])
+    skip_x.start(off_plane)
+    loads["k_out"].wait()
+    for k in range(9):
+        turns = []
+        for dz in range(3):
+            block = b["k_out"][64 * (3 * k + dz) : 64 * (3 * k + dz) + 64, :]
+            turns.append(turned(jnp.concatenate([block, block], axis=0)))
+        band(lambda dz: turns[dz][0:64], b["t_lift"], k, 0)
+        band(lambda dz: turns[dz][64:128], b["t_skip"], k)
+    loads["raw_ll"].wait()
+    for q in range(0, 256, 64):
+        raw = b["raw_ll"][q : q + 64].astype(F32)
+        for i in range(4):
+            for k in range(2):
+                b["k_ll"][q : q + 64, tile(2 * i + k)] = raw[:, i, k, :].astype(BF16)
     loads["k_um"].wait()
     for half in range(2):
         for k in range(9):
@@ -485,30 +496,35 @@
             cell = first_mid[at : at + 16, tile(z % 2)]
             fm_wide[x, z, 0:16, :] = jnp.where(mid_rows, cell, 0.0) * keep
 
-    def gather(wide_ref, target, xs, pairs, lanes):
+    def gather(wide_ref, target, xs, count):
         for x in range(xs):
-            for zp in range(pairs):
-                for dy in range(3):
-                    for dz in range(3):
+            for dy in range(3):
+                for odd in range(2):
+                    for zp in range(count + 1 - odd):
+                        z = 2 * zp + odd
                         both = jnp.concatenate(
-                            [wide_ref[x, 2 * zp + h + dz, dy : dy + 8, :] for h in range(2)], axis=0
+                            [wide_ref[x, z + h, dy : dy + 8, :] for h in range(2)], axis=0
                         )
-                        at = (3 * dy + dz) * lanes
-                        target[x, 16 * zp : 16 * zp + 16, at : at + lanes] = both.astype(BF16)
-
-    def conv_rows(source, xs, kernels):
-        rows, depth = source.shape[1], source.shape[2]
+                        target[odd, dy, x, 16 * zp : 16 * zp + 16, :] = both.astype(BF16)
+
+    def conv_rows(source, xs, count, kernels):
         total = None
         for dx in range(3):
-            piece = source[dx : dx + xs].reshape(xs * rows, depth)
-            term = dot(piece, kernels[dx * depth : (dx + 1) * depth, :])
+            pieces = []
+            for dy in range(3):
+                for dz in range(3):
+                    first = 16 * (dz // 2)
+                    piece = source[dz % 2, dy, dx : dx + xs, first : first + 16 * count, :]
+                    pieces.append(piece.reshape(xs * 16 * count, source.shape[4]))
+            depth = 9 * source.shape[4]
+            term = dot(jnp.concatenate(pieces, axis=1), kernels[dx * depth : (dx + 1) * depth, :])
             total = term if total is None else total + term
         return jnp.maximum(total, 0.0)
 
-    gather(fm_wide, b["fm_s"], 6, 4, 128)
+    gather(fm_wide, b["fm_s"], 6, 4)
     loads["k_db"].wait()
     sm_out, sm = b["sm_out"], b["sm"]
-    skip_mid = conv_rows(b["fm_s"], 4, b["k_db"])
+    skip_mid = conv_rows(b["fm_s"], 4, 4, b["k_db"])
     sm_out[...] = skip_mid.reshape(4, 8, 8, 128)
     sm[2:6, 1:5] = skip_mid.astype(BF16).reshape(4, 4, 16, 128)
 
@@ -639,9 +655,9 @@
                 pl_wide[x, to, 0:3, :] = pl_g[0, 4 * z + 1 : 4 * z + 4, :]
                 pl_wide[x, to, 3:7, :] = pl_g[1, 4 * z : 4 * z + 4, :]
                 pl_wide[x, to, 7:10, :] = pl_g[2, 4 * z : 4 * z + 3, :]
-    gather(pl_wide, b["pl_s"], 8, 4, 128)
+    gather(pl_wide, b["pl_s"], 8, 4)
     loads["k_la"].wait()
-    first_low = conv_rows(b["pl_s"], 6, b["k_la"])
+    first_low = conv_rows(b["pl_s"], 6, 4, b["k_la"])
     fl_wide = b["fl_wide"]
     low_rows = row_mask(8, 256, 8, gy, 4, sizes[1], -2)
     for x in range(6):
@@ -650,9 +666,9 @@
             at = 64 * x + 8 * z
             fl_wide[x, z, 0:8, :] = jnp.where(low_rows, first_low[at : at + 8, :], 0.0) * keep
             fl_wide[x, z, 8:16, :] = jnp.zeros((8, 256), F32)
-    gather(fl_wide, b["fl_s"], 6, 3, 256)
+    gather(fl_wide, b["fl_s"], 6, 3)
     loads["k_lb"].wait()
-    coarse = conv_rows(b["fl_s"], 4, b["k_lb"])
+    coarse = conv_rows(b["fl_s"], 4, 3, b["k_lb"])
     coarse_rows = row_mask(8, 256, 6, gy, 4, sizes[1], -1)
     cells = []
     for x in range(4):

time: 41.7 us -> 40.9 us (0.981)
  Pallas kernels: 40.9 us -> 40.1 us
    pallas_call x1, Pallas kernels: 40.9 us -> 40.1 us  [body(): pl.pallas_call(functools.partial(kernel, sizes), out_shape=pltpu.VMEM(vol...]
where the time goes in v5:
time: 40.9 us; the launch traced here: 40.8 us
  Pallas kernels  40.1 us (98%)
  local copies, waits for them, and re-layouts  0.71 us (2%)
    pallas_call x1, Pallas kernels, body(): pl.pallas_call(functools.partial(kernel, sizes), out_shape=pltpu.VMEM(vol...  40.1 us

profile of v5, /device:TPU:1, one launch (start us, length us, event | category | flops | bytes accessed | tf_op | source)
XLA Modules:
  0.0 40.8 jit_solution(15141229551864200759)
XLA Ops:
  0.0 40.1 %shard_map.100 = bf16[8,16,1024]{2,1,0:T(8,128)(2,1)S(1)} custom-call(bf16[8,16,1024]{2,1,0:T(8,128)(2,1)} %refs_0_.1, bf16[1728,64]{1,0:T(8,128)(2,1)} %bitcast.18, bf16[1728,128]{1,0:T(8,128)(2,1)} %bitcast.19, bf16[3456,128]{1,0:T(8,128)(2,1)} %bitcast.16, bf16[3456,256]{1,0:T(8,128)(2,1)} %bitcast.14, bf16[6912,256]{1,0:T(8,128)(2,1)} %bitcast.13, ...), custom_call_target="tpu_custom_call" | custom-call | tf_op jit(solution)/shard_map/pallas_call | solution.py:743
  40.1 0.7 %copy.12 = bf16[8,16,1024]{2,1,0:T(8,128)(2,1)} copy(bf16[8,16,1024]{2,1,0:T(8,128)(2,1)S(1)} %shard_map.100) | data formatting | bytes 524288

commit v6 on v5

--- a/solution.py
+++ b/solution.py
@@ -338,8 +338,6 @@
     )
     pl.semaphore_wait(barrier, greeted)
     vol_x.start()
-    mg_wide = b["mg_wide"]
-    zero(mg_wide)
     loads["k_top"].wait()
     for k in range(9):
 
@@ -430,15 +428,6 @@
         for i in range(4):
             for k in range(2):
                 b["k_ll"][q : q + 64, tile(2 * i + k)] = raw[:, i, k, :].astype(BF16)
-    loads["k_um"].wait()
-    for half in range(2):
-        for k in range(9):
-
-            def up_block(dz, half=half, k=k):
-                at = 256 * (3 * k + dz) + 128 * half
-                return b["k_um"][at : at + 128, :]
-
-            pairs(up_block, 4, 128, b["t_um"].at[half, k])
     pm_x.wait_recv()
     for xp in range(4):
         for zp in range(6):
@@ -579,7 +568,7 @@
         xs = {0: slice(0, 4), 1: slice(2, 4), -1: slice(0, 2)}[dx]
         return b["sm_y"].at[s, xs], b["sm_r"].at[s, dx + 1, xs]
 
-    sm_x = Exchange(DIRS, sm_message, sm_ss, sm_rs, here, sizes)
+    sm_x = Exchange(DIRS[::-1], sm_message, sm_ss, sm_rs, here, sizes)
     sm_x.start()
 
     skip_x.wait_recv()
@@ -588,6 +577,17 @@
     b["part"][...] = conv_top((b["skip0"], skip1, b["skip2"]), b["t_skip"])
     line_x.wait_recv()
     pl_x.start()
+    loads["k_um"].wait()
+    for half in range(2):
+        for k in range(9):
+
+            def up_block(dz, half=half, k=k):
+                at = 256 * (3 * k + dz) + 128 * half
+                return b["k_um"][at : at + 128, :]
+
+            pairs(up_block, 4, 128, b["t_um"].at[half, k])
+    mg_wide = b["mg_wide"]
+    zero(mg_wide)
 
     t_lt = b["t_lt"]
     loads["k_lt"].wait()

time: 40.9 us -> 40.9 us (level)
  no operation moved by 1% of the time
where the time goes in v6:
time: 40.9 us; the launch traced here: 40.8 us
  Pallas kernels  40.1 us (98%)
  local copies, waits for them, and re-layouts  0.71 us (2%)
    pallas_call x1, Pallas kernels, body(): pl.pallas_call(functools.partial(kernel, sizes), out_shape=pltpu.VMEM(vol...  40.1 us

profile of v6, /device:TPU:1, one launch (start us, length us, event | category | flops | bytes accessed | tf_op | source)
XLA Modules:
  0.0 40.8 jit_solution(12341020323456229481)
XLA Ops:
  0.0 40.1 %shard_map.100 = bf16[8,16,1024]{2,1,0:T(8,128)(2,1)S(1)} custom-call(bf16[8,16,1024]{2,1,0:T(8,128)(2,1)} %refs_0_.1, bf16[1728,64]{1,0:T(8,128)(2,1)} %bitcast.18, bf16[1728,128]{1,0:T(8,128)(2,1)} %bitcast.19, bf16[3456,128]{1,0:T(8,128)(2,1)} %bitcast.16, bf16[3456,256]{1,0:T(8,128)(2,1)} %bitcast.14, bf16[6912,256]{1,0:T(8,128)(2,1)} %bitcast.13, ...), custom_call_target="tpu_custom_call" | custom-call | tf_op jit(solution)/shard_map/pallas_call | solution.py:743
  40.1 0.7 %copy.12 = bf16[8,16,1024]{2,1,0:T(8,128)(2,1)} copy(bf16[8,16,1024]{2,1,0:T(8,128)(2,1)S(1)} %shard_map.100) | data formatting | bytes 524288
